TPU v7x, 256 devices: a whole 4x4x8 slice. The times are simulated.
256 devices in a mesh: pool: 4 (over y), ep: 64 (over z, x, core).
Axes of the slice: x: 4, y: 4, z: 8, core: 2. Of those that a mesh axis runs over, the one named last changes fastest.
Arguments:
- residual: bfloat16 [2048, 4096], P(('pool', 'ep')), may hold values from -6 to 6
- queries: bfloat16 [2048, 8192], P(('pool', 'ep')), may hold values from -6 to 6
- token_keys: bfloat16 [2048, 512], P(('pool', 'ep')), may hold values from -6 to 6
- token_values: bfloat16 [2048, 512], P(('pool', 'ep')), may hold values from -6 to 6
- resident_cache: bfloat16 [2048, 2, 64, 512], P(('pool', 'ep')), may hold values from -6 to 6
- pool_block_cache: bfloat16 [64, 128, 2, 16, 512], P('ep', 'pool'), may hold values from -6 to 6
- block_table: int32 [2048, 4], P(('pool', 'ep')), may hold values from 0 to 127, as said below
- resumed: int32 [2048], P(('pool', 'ep')), may hold values from 0 to 1, as said below
- lengths: int32 [2048], P(('pool', 'ep')), may hold values from 2 to 64
- out_proj: bfloat16 [8192, 4096], P('ep'), may hold values from -0.0625 to 0.0625
- norm_gain: bfloat16 [4096], replicated, may hold values from 0.25 to 1.75
- expert_ids: int32 [2048, 8], P(('pool', 'ep')), may hold values from 0 to 63, all different within a row; in each aligned block of 8 rows (0 to 7, 8 to 15, ...) at most 2 rows name the same one
- route_scores: float32 [2048, 8], P(('pool', 'ep')), may hold values from 0.05 to 1
- expert_gate: bfloat16 [64, 4096, 1536], P('ep', None, 'pool'), may hold values from -0.09375 to 0.09375
- expert_up: bfloat16 [64, 4096, 1536], P('ep', None, 'pool'), may hold values from -0.09375 to 0.09375
- expert_down: bfloat16 [64, 1536, 4096], P('ep', 'pool'), may hold values from -0.15625 to 0.15625
Outputs:
- attended: bfloat16 [2048, 4096], P(('pool', 'ep'))
- layer_out: bfloat16 [2048, 4096], P(('pool', 'ep'))
Inputs may be any that keep to these rules, and one draw needn't show every extreme that they name: `block_table`: entry // 32 is the pool index that holds the block, within the pool of the row's ep index; every row has 1 of its blocks on each pool index. At most 4 rows of one device are resumed; the first device has exactly 4. `expert_ids`: among the rows of one device no expert is named more than 2 times, a bound that some block reaches.
All inputs are finite; a program needn't handle non-finite values.
Results may differ from a plain program's by a relative error of at most 0.012.
Values may be sent and summed in bfloat16 or wider, within the bound.
No kernel may reach another device: no remote copies, remote signals or barrier semaphores. Data moves between devices by JAX's collectives and lax.ppermute only.
A program may use at most 128 MiB of HBM per device.

v0:
```python
import functools
import math

import jax
import jax.numpy as jnp
import numpy as np
from jax import lax
from jax.experimental import pallas as pl
from jax.experimental.pallas import tpu as pltpu
from jax.sharding import PartitionSpec as P

D = 4096
QUERY_HEADS = 64
KEY_VALUE_HEADS = 4
GROUP = QUERY_HEADS // KEY_VALUE_HEADS
HEAD_SIZE = 128
WIDE = KEY_VALUE_HEADS * HEAD_SIZE
CONTEXT_LIMIT = 64
BLOCK_POSITIONS = 16
RES_MOST = 4
CAP = 2
ROWS = 8
FACTS = 7
N_POOL = 4
N_Z, N_X, N_CORE = 8, 4, 2
N_PLANE = N_X * N_CORE
N_EP = N_Z * N_PLANE
DEEP = N_PLANE * HEAD_SIZE
CHUNK = D // N_PLANE
PARTS = 4
PART = D // PARTS
FF_PART = 384
STEPS = 2
PER_STEP = PARTS // STEPS
HALF = N_EP // 2 * PARTS * CAP
NORM_EPSILON = 1e-06
NEG_FILL = -1e30
BIG = 48 * 1024 * 1024
MOST = 60 * 1024 * 1024


def shift_pool(value, step):
    return lax.ppermute(value, "pool", [(i, (i + step) % N_POOL) for i in range(N_POOL)])


def shift_ep(value, x=0, core=0):
    pairs = []
    for i in range(N_EP):
        a, b, c = i // N_PLANE, i // N_CORE % N_X, i % N_CORE
        pairs.append((i, a * N_PLANE + (b + x) % N_X * N_CORE + (c + core) % N_CORE))
    return lax.ppermute(value, "ep", pairs)


def whole(shape):
    return pl.BlockSpec(shape, lambda *_: (0,) * len(shape))


def gather_kernel(*refs):
    asked, cache_ref = refs[:N_POOL], refs[N_POOL]
    outs, (slot_ref, sems) = refs[N_POOL + 1 : 2 * N_POOL + 1], refs[2 * N_POOL + 1 :]
    for i in range(N_POOL * RES_MOST):
        slot_ref[i] = 0
    for d in range(N_POOL):
        count = 0
        for row in range(ROWS):
            wanted = asked[d][row]
            at = d * RES_MOST + jnp.minimum(count, RES_MOST - 1)

            @pl.when(wanted >= 0)
            def _(wanted=wanted, at=at):
                slot_ref[at] = jnp.minimum(wanted, cache_ref.shape[0] - 1)

            count = count + jnp.where(wanted >= 0, 1, 0)
    copies = []
    for d in range(N_POOL):
        for j in range(RES_MOST):
            at = d * RES_MOST + j
            copy = pltpu.make_async_copy(cache_ref.at[slot_ref[at]], outs[d].at[j], sems.at[at])
            copy.start()
            copies.append(copy)
    for copy in copies:
        copy.wait()


def fetch_blocks(cache, block_table, resumed, lengths, queries, pool):
    slots = cache.shape[0]
    live = resumed > 0
    holder = block_table // slots
    within = block_table % slots
    from_me = (pool + jnp.arange(N_POOL)) % N_POOL
    at_holder = holder[None] == from_me[:, None, None]
    wanted = jnp.sum(jnp.where(at_holder, within[None], 0), axis=2)
    wanted = jnp.where(live[None, :], wanted, -1)
    asked = [wanted[0]] + [shift_pool(wanted[d], d) for d in range(1, N_POOL)]
    row = jnp.arange(ROWS)
    rank = jnp.sum(jnp.where(row[None, :] < row[:, None], resumed[None, :], 0), axis=1)
    rank = jnp.clip(rank, 0, RES_MOST - 1)
    start = jnp.arange(N_POOL) * BLOCK_POSITIONS
    place = jnp.sum(jnp.where(at_holder, start[None, None, :], 0), axis=2).T
    place = jnp.where(live[:, None], place, start[None, :])
    facts = jnp.concatenate([rank[:, None], resumed[:, None], lengths[:, None], place], axis=1).reshape(-1)
    queries = queries.reshape(ROWS, QUERY_HEADS, HEAD_SIZE)
    *asked, facts, queries = lax.optimization_barrier((*asked, facts, queries))
    shape = jax.ShapeDtypeStruct((RES_MOST,) + cache.shape[1:], jnp.bfloat16)
    gathered = pl.pallas_call(
        gather_kernel,
        grid_spec=pltpu.PrefetchScalarGridSpec(
            num_scalar_prefetch=N_POOL,
            grid=(1,),
            in_specs=[pl.BlockSpec(memory_space=pl.ANY)],
            out_specs=[whole(shape.shape)] * N_POOL,
            scratch_shapes=[
                pltpu.SMEM((N_POOL * RES_MOST,), jnp.int32),
                pltpu.SemaphoreType.DMA((N_POOL * RES_MOST,)),
            ],
        ),
        out_shape=[shape] * N_POOL,
        cost_estimate=pl.CostEstimate(flops=0, bytes_accessed=1 << 20, transcendentals=0),
    )(*asked, cache)
    blocks = [gathered[0]] + [shift_pool(gathered[d], -d) for d in range(1, N_POOL)]
    return blocks, facts, queries


def attention_kernel(facts_ref, query_ref, key_ref, value_ref, resident_ref, b0, b1, b2, b3, out_ref):
    wider = CONTEXT_LIMIT + 16
    lane = lax.broadcasted_iota(jnp.int32, (1, wider), 1)
    head_of = lax.broadcasted_iota(jnp.int32, (QUERY_HEADS, WIDE), 0) // GROUP
    block_of = lax.broadcasted_iota(jnp.int32, (QUERY_HEADS, WIDE), 1) // HEAD_SIZE
    diagonal = head_of == block_of
    first = lax.broadcasted_iota(jnp.int32, (16, WIDE), 0) == 0
    factor = 1.0 / math.sqrt(HEAD_SIZE)
    results = []
    for row in range(ROWS):
        rank, resumed, length, *place = [facts_ref[row * FACTS + i] for i in range(FACTS)]
        is_resumed = resumed > 0

        def of_kind(kind, own_ref):
            loaded = jnp.concatenate([b[rank, kind] for b in (b0, b1, b2, b3)], axis=0)
            cached = jnp.where(is_resumed, loaded, resident_ref[row, kind])
            own = jnp.where(first, own_ref[row : row + 1, :].astype(jnp.float32), 0.0)
            return jnp.concatenate([cached, own.astype(jnp.bfloat16)], axis=0)

        keys, values = of_kind(0, key_ref), of_kind(1, value_ref)
        position = lane % BLOCK_POSITIONS
        for i in range(N_POOL):
            position = position + jnp.where(lane // BLOCK_POSITIONS == i, place[i], 0)
        live = ((lane < CONTEXT_LIMIT) & (position < length)) | (lane == CONTEXT_LIMIT)
        query = query_ref[row]
        query = jnp.where(diagonal, jnp.concatenate([query] * KEY_VALUE_HEADS, axis=1), 0)
        scores = lax.dot_general(
            query.astype(jnp.bfloat16), keys, (((1,), (1,)), ((), ())), preferred_element_type=jnp.float32
        )
        scores = jnp.where(live, scores * factor, NEG_FILL)
        highest = jnp.max(scores, axis=1, keepdims=True)
        raised = jnp.where(live, jnp.exp(scores - highest), 0.0)
        weights = (raised / jnp.sum(raised, axis=1, keepdims=True)).astype(jnp.bfloat16)
        spread = jnp.dot(weights, values, preferred_element_type=jnp.float32)
        results.append(
            jnp.concatenate(
                [
                    spread[k * GROUP : (k + 1) * GROUP, k * HEAD_SIZE : (k + 1) * HEAD_SIZE]
                    for k in range(KEY_VALUE_HEADS)
                ],
                axis=0,
            )
        )
    by_head = jnp.swapaxes(jnp.stack(results), 0, 1)
    planes = [
        jnp.concatenate([by_head[z * N_PLANE + h] for h in range(N_PLANE)], axis=1) for z in range(N_Z)
    ]
    out_ref[...] = jnp.concatenate(planes, axis=0).astype(jnp.bfloat16)


def attend(queries, token_keys, token_values, resident, blocks, facts):
    block = whole(blocks[0].shape)
    sent = N_Z * ROWS
    return pl.pallas_call(
        attention_kernel,
        grid_spec=pltpu.PrefetchScalarGridSpec(
            num_scalar_prefetch=1,
            grid=(1,),
            in_specs=[
                whole((ROWS, QUERY_HEADS, HEAD_SIZE)),
                whole((ROWS, WIDE)),
                whole((ROWS, WIDE)),
                whole(resident.shape),
                block,
                block,
                block,
                block,
            ],
            out_specs=whole((sent, DEEP)),
        ),
        out_shape=jax.ShapeDtypeStruct((sent, DEEP), jnp.bfloat16),
        compiler_params=pltpu.CompilerParams(vmem_limit_bytes=MOST),
        cost_estimate=pl.CostEstimate(flops=1 << 28, bytes_accessed=3 << 20, transcendentals=1 << 16),
    )(
        facts, queries, token_keys, token_values, resident, *blocks
    )


def pair_projection(out_proj, core):
    columns = N_X * CHUNK
    mine = lax.dynamic_slice_in_dim(out_proj, core * columns, columns, 1)
    other = lax.dynamic_slice_in_dim(out_proj, (1 - core) * columns, columns, 1)
    came = shift_ep(other, core=1)
    both = jnp.where(core == 0, jnp.stack([mine, came]), jnp.stack([came, mine]))
    return both.reshape(N_CORE * HEAD_SIZE, columns)


def cut_projection(pair, x):
    return [lax.dynamic_slice_in_dim(pair, (x + d) % N_X * CHUNK, CHUNK, 1) for d in range(N_X)]


def join_kernel(*refs):
    refs[-1][...] = jnp.concatenate([r[...] for r in refs[:-1]], axis=0)


def project_kernel(at_ref, mine_ref, other_ref, w0, w1, w2, w3, out_ref):
    x, core = at_ref[0], at_ref[1]
    width = N_CORE * HEAD_SIZE
    rows = N_Z * ROWS
    total = jnp.zeros((2 * N_X * rows, CHUNK), jnp.float32)
    for d, w_ref in enumerate((w0, w1, w2, w3)):
        source = (x + N_X - d) % N_X
        columns = pl.ds(pl.multiple_of(source * width, width), width)
        taken = jnp.concatenate([mine_ref[:, columns], other_ref[:, columns]], axis=0)
        total = total + jnp.dot(taken, w_ref[...], preferred_element_type=jnp.float32)
    for d in range(N_X):
        mine = total[d * rows : (d + 1) * rows].reshape(N_Z, ROWS, CHUNK)
        other = total[(N_X + d) * rows : (N_X + d + 1) * rows].reshape(N_Z, ROWS, CHUNK)
        first = jnp.where(core == 0, mine, other)
        second = jnp.where(core == 0, other, mine)
        both = jnp.concatenate([first, second], axis=1).astype(jnp.bfloat16)
        out_ref[:, pl.ds((x + N_X - d) % N_X, 1)] = both.reshape(N_Z, 1, N_CORE * ROWS, CHUNK)


def project(context, pieces, x, core):
    columns = [[z * N_PLANE + i for z in range(N_Z)] for i in range(N_PLANE)]
    local = lax.all_to_all(
        context.reshape(N_Z, ROWS, DEEP),
        "ep", split_axis=0, concat_axis=0, axis_index_groups=columns, tiled=True,
    ).reshape(N_Z * ROWS, DEEP)
    local, *pieces = lax.optimization_barrier((local, *pieces))
    far = [shift_ep(local, x=d) for d in range(1, N_X)]
    mine = pl.pallas_call(
        join_kernel,
        out_shape=jax.ShapeDtypeStruct((N_X * N_Z * ROWS, DEEP), jnp.bfloat16),
        compiler_params=pltpu.CompilerParams(vmem_limit_bytes=BIG),
    )(local, *far)
    operands = [mine, shift_ep(mine, core=1), *pieces]
    shape = (N_Z, N_X, N_CORE * ROWS, CHUNK)
    product = pl.pallas_call(
        project_kernel,
        grid_spec=pltpu.PrefetchScalarGridSpec(
            num_scalar_prefetch=1,
            grid=(1,),
            in_specs=[whole(a.shape) for a in operands],
            out_specs=whole(shape),
        ),
        out_shape=jax.ShapeDtypeStruct(shape, jnp.bfloat16),
        compiler_params=pltpu.CompilerParams(vmem_limit_bytes=BIG),
    )(jnp.stack([x, core]).astype(jnp.int32), *operands)
    summands = lax.all_to_all(
        product.reshape(N_EP, ROWS, CHUNK), "ep", split_axis=0, concat_axis=0, tiled=True
    )
    return summands.reshape(N_EP * ROWS, CHUNK)


def dispatch_kernel(summand_ref, residual_ref, gain_ref, pick_ref, attended_ref, out_ref):
    total = summand_ref[...].astype(jnp.float32).reshape(N_Z, N_PLANE * ROWS, CHUNK).sum(axis=0)
    columns = []
    for chunk in range(N_PLANE):
        source = chunk % N_X * N_CORE + chunk // N_X
        columns.append(total[source * ROWS : (source + 1) * ROWS])
    projected = jnp.concatenate(columns, axis=1)
    attended = (residual_ref[...].astype(jnp.float32) + projected).astype(jnp.bfloat16)
    attended_ref[...] = attended
    widened = attended.astype(jnp.float32)
    mean = jnp.sum(widened * widened, axis=1, keepdims=True) * (1.0 / D)
    normed = widened * lax.rsqrt(mean + NORM_EPSILON) * gain_ref[...].astype(jnp.float32)
    stacked = jnp.concatenate([normed[:, j * PART : (j + 1) * PART] for j in range(PARTS)], axis=0)
    out_ref[...] = jnp.dot(
        pick_ref[...], stacked.astype(jnp.bfloat16), preferred_element_type=jnp.float32
    ).astype(jnp.bfloat16)


def expert_kernel(layout, order_ref, *refs):
    count = len(layout)
    ins, (gate_ref, up_ref, down_ref) = refs[:count], refs[count : count + 3]
    outs = refs[count + 3 : 2 * count + 3]
    tokens, gate_sum, up_sum, hidden, results = refs[2 * count + 3 :]
    halves = [(i, h) for i, n in enumerate(layout) for h in range(n)]
    per_half = HALF // PARTS
    step = pl.program_id(0)

    @pl.when(step == 0)
    def _():
        for at, (i, h) in enumerate(halves):
            block = jnp.dot(
                order_ref[...], ins[i][h * HALF : (h + 1) * HALF, :], preferred_element_type=jnp.float32
            ).astype(jnp.bfloat16)
            for j in range(PARTS):
                tokens[j, at * per_half : (at + 1) * per_half, :] = block[j * per_half : (j + 1) * per_half]

    @pl.when(step < STEPS)
    def _():
        gate = jnp.where(step == 0, 0.0, gate_sum[...])
        up = jnp.where(step == 0, 0.0, up_sum[...])
        for at in range(PER_STEP):
            part = tokens[jnp.minimum(step, STEPS - 1) * PER_STEP + at]
            depth = slice(at * PART, (at + 1) * PART)
            gate = gate + jnp.dot(part, gate_ref[depth, :], preferred_element_type=jnp.float32)
            up = up + jnp.dot(part, up_ref[depth, :], preferred_element_type=jnp.float32)
        gate_sum[...], up_sum[...] = gate, up

    @pl.when(step == STEPS)
    def _():
        gate = gate_sum[...]
        hidden[...] = (gate * (1.0 / (1.0 + jnp.exp(-gate))) * up_sum[...]).astype(jnp.bfloat16)

    @pl.when(step >= STEPS)
    def _():
        for at in range(PER_STEP):
            results[jnp.maximum(step - STEPS, 0) * PER_STEP + at] = jnp.dot(
                hidden[...], down_ref[:, at * PART : (at + 1) * PART], preferred_element_type=jnp.float32
            ).astype(jnp.bfloat16)

    @pl.when(step == 2 * STEPS - 1)
    def _():
        for at, (i, h) in enumerate(halves):
            block = jnp.concatenate(
                [results[j, at * per_half : (at + 1) * per_half, :] for j in range(PARTS)], axis=0
            )
            outs[i][h * HALF : (h + 1) * HALF, :] = lax.dot_general(
                order_ref[...], block, (((0,), (0,)), ((), ())), preferred_element_type=jnp.float32
            ).astype(jnp.bfloat16)


def expert(arrays, w_gate, w_up, w_down, order):
    layout = [a.shape[0] // HALF for a in arrays]
    rows = sum(layout) * HALF // PARTS
    span = PER_STEP * PART
    gate_spec = pl.BlockSpec((span, FF_PART), lambda i: (jnp.minimum(i, STEPS - 1), 0))
    down_spec = pl.BlockSpec((FF_PART, span), lambda i: (0, jnp.maximum(i - STEPS, 0)))
    return pl.pallas_call(
        functools.partial(expert_kernel, layout),
        grid=(2 * STEPS,),
        in_specs=[whole(order.shape)] + [whole(a.shape) for a in arrays] + [gate_spec, gate_spec, down_spec],
        out_specs=[whole(a.shape) for a in arrays],
        out_shape=[jax.ShapeDtypeStruct(a.shape, jnp.bfloat16) for a in arrays],
        scratch_shapes=[
            pltpu.VMEM((PARTS, rows, PART), jnp.bfloat16),
            pltpu.VMEM((rows, FF_PART), jnp.float32),
            pltpu.VMEM((rows, FF_PART), jnp.float32),
            pltpu.VMEM((rows, FF_PART), jnp.bfloat16),
            pltpu.VMEM((PARTS, rows, PART), jnp.bfloat16),
        ],
        compiler_params=pltpu.CompilerParams(vmem_limit_bytes=BIG),
        cost_estimate=pl.CostEstimate(
            flops=6 * rows * D * FF_PART, bytes_accessed=6 * D * FF_PART + 4 * rows * D, transcendentals=0
        ),
    )(order, *arrays, w_gate, w_up, w_down)


def sum_kernel(base_a_ref, base_b_ref, right_ref, left_ref, out_ref):
    out_ref[:HALF, :] = (base_a_ref[...] + right_ref[...].astype(jnp.float32)).astype(jnp.bfloat16)
    out_ref[HALF:, :] = (base_b_ref[...] + left_ref[...].astype(jnp.float32)).astype(jnp.bfloat16)


def finish_kernel(mix_ref, returned_ref, attended_ref, out_ref):
    summed = jnp.dot(mix_ref[...], returned_ref[...], preferred_element_type=jnp.float32)
    wide = PARTS * ROWS
    summed = summed[:wide] + summed[wide : 2 * wide] + summed[2 * wide :]
    mixture = jnp.concatenate([summed[j * ROWS : (j + 1) * ROWS] for j in range(PARTS)], axis=1)
    out_ref[...] = (attended_ref[...].astype(jnp.float32) + mixture).astype(jnp.bfloat16)


def routes(expert_ids, route_scores):
    shares = route_scores / jnp.sum(route_scores, axis=1, keepdims=True)
    named = expert_ids[:, :, None] == jnp.arange(N_EP)[None, None, :]
    hit = jnp.any(named, axis=1)
    share = jnp.sum(jnp.where(named, shares[:, :, None], 0.0), axis=1)
    row = jnp.arange(ROWS)
    earlier = row[None, :, None] < row[:, None, None]
    before = jnp.sum(jnp.where(earlier & hit[None], 1, 0), axis=1)
    slot = hit[:, :, None] & (before[:, :, None] == jnp.arange(CAP))
    same = jnp.arange(PARTS)[:, None] == jnp.arange(PARTS)[None, :]
    pick = jnp.where(
        slot.transpose(1, 2, 0)[:, None, :, None, :] & same[None, :, None, :, None], 1.0, 0.0
    ).reshape(N_EP * PARTS * CAP, PARTS * ROWS)
    mix = jnp.where(
        slot[None, :, :, None, :] & same[:, None, None, :, None], share[None, :, :, None, None], 0.0
    ).reshape(PARTS * ROWS, N_EP * PARTS * CAP)
    high = lax.reduce_precision(mix, 8, 7)
    middle = lax.reduce_precision(mix - high, 8, 7)
    low = mix - high - middle
    return pick.astype(jnp.bfloat16), jnp.concatenate([high, middle, low]).astype(jnp.bfloat16)


def order_matrix():
    half = N_EP // 2
    message = np.arange(HALF).reshape(half, PARTS, CAP)
    token = message.transpose(1, 0, 2).reshape(-1)
    return (token[:, None] == np.arange(HALF)[None, :]).astype(jnp.bfloat16)


def shards(
    residual,
    queries,
    token_keys,
    token_values,
    resident_cache,
    pool_block_cache,
    block_table,
    resumed,
    lengths,
    out_proj,
    norm_gain,
    expert_ids,
    route_scores,
    expert_gate,
    expert_up,
    expert_down,
):
    pool = lax.axis_index("pool")
    ep = lax.axis_index("ep")
    x, core = ep // N_CORE % N_X, ep % N_CORE

    blocks, facts, heads = fetch_blocks(
        pool_block_cache[0], block_table, resumed, lengths, queries, pool
    )
    pair = pair_projection(out_proj, core)
    pick, mix = routes(expert_ids, route_scores)
    blocks[1], pair, facts, heads = lax.optimization_barrier((blocks[1], pair, facts, heads))
    cuts = cut_projection(pair, x)
    pieces = [cuts[0]] + [shift_ep(cuts[d], x=d) for d in range(1, N_X)]
    context = attend(heads, token_keys, token_values, resident_cache, blocks, facts)
    summands = project(context, pieces, x, core)
    message = (N_EP * PARTS * CAP, PART)
    attended, outgoing = pl.pallas_call(
        dispatch_kernel,
        out_shape=[
            jax.ShapeDtypeStruct((ROWS, D), jnp.bfloat16),
            jax.ShapeDtypeStruct(message, jnp.bfloat16),
        ],
        compiler_params=pltpu.CompilerParams(vmem_limit_bytes=BIG),
    )(summands, residual, norm_gain.reshape(1, D), pick)

    def exchange(rows):
        parted = rows.reshape(N_EP, PARTS * CAP, PART)
        return lax.all_to_all(parted, "ep", split_axis=0, concat_axis=0, tiled=True).reshape(message)

    weights = (expert_gate[0], expert_up[0], expert_down[0], jnp.asarray(order_matrix()))
    mine = exchange(outgoing)
    left, right = shift_pool(mine, 1), shift_pool(mine, -1)
    (own,) = expert([mine], *weights)
    left, right, own = lax.optimization_barrier((left, right, own))
    far_a, far_b = shift_pool(right[:HALF], -1), shift_pool(left[HALF:], 1)
    to_left, to_right = expert([left, right], *weights)
    right_b, left_a = shift_pool(to_right[HALF:], 1), shift_pool(to_left[:HALF], -1)
    far_a, far_b, to_left, to_right = lax.optimization_barrier((far_a, far_b, to_left, to_right))
    to_far_a, to_far_b = expert([far_a, far_b], *weights)
    over_a, over_b = shift_pool(to_far_a, 1), shift_pool(to_far_b, -1)

    def wide(value):
        return value.astype(jnp.float32)

    base_a, base_b = wide(own[:HALF]) + wide(left_a), wide(own[HALF:]) + wide(right_b)
    over_a, over_b, base_a, base_b = lax.optimization_barrier((over_a, over_b, base_a, base_b))
    right_a = shift_pool((wide(to_right[:HALF]) + wide(over_a)).astype(jnp.bfloat16), 1)
    left_b = shift_pool((wide(to_left[HALF:]) + wide(over_b)).astype(jnp.bfloat16), -1)
    summed = pl.pallas_call(
        sum_kernel,
        out_shape=jax.ShapeDtypeStruct(message, jnp.bfloat16),
        compiler_params=pltpu.CompilerParams(vmem_limit_bytes=BIG),
    )(base_a, base_b, right_a, left_b)
    returned = exchange(summed)
    layer_out = pl.pallas_call(
        finish_kernel,
        out_shape=jax.ShapeDtypeStruct((ROWS, D), jnp.bfloat16),
        compiler_params=pltpu.CompilerParams(vmem_limit_bytes=BIG),
    )(mix, returned, attended)
    return (attended, layer_out)


def solution(mesh):
    placed = (
        P(("pool", "ep"), None),
        P(("pool", "ep"), None),
        P(("pool", "ep"), None),
        P(("pool", "ep"), None),
        P(("pool", "ep"), None, None, None),
        P("ep", "pool", None, None, None),
        P(("pool", "ep"), None),
        P(("pool", "ep")),
        P(("pool", "ep")),
        P("ep", None),
        P(),
        P(("pool", "ep"), None),
        P(("pool", "ep"), None),
        P("ep", None, "pool"),
        P("ep", None, "pool"),
        P("ep", "pool", None),
    )
    return jax.shard_map(
        shards,
        mesh=mesh,
        in_specs=placed,
        out_specs=(P(("pool", "ep"), None), P(("pool", "ep"), None)),
        check_vma=False,
    )
```

profile of v0, /device:TPU:24, one launch (start us, length us, event | category | flops | bytes accessed | tf_op | source)
XLA Modules:
  0.0 242.8 jit_solution(8827355356747572559)
XLA Ops:
  0.7 1.3 dynamic-slice_bitcast_fusion
  2.0 0.7 broadcast_compare_fusion.1
  2.7 0.7 add_select_fusion
  3.6 0.5 slice_bitcast_fusion
  4.1 0.7 collective-permute-start.2
  4.8 2.7 %collective-permute-start.1 = (s32[8]{0:T(128)S(1)}, s32[8]{0:T(128)S(1)}, u32[]{:S(2)}, u32[]{:S(2)}) collective-permute-start(s32[8]{0:T(128)S(1)} %get-tuple-element.88), channel_id=1, source_target_pairs={{0,128},{64,192},{128,0},{192,64},{1,129},{65,193},{129,1},{193,65... | collective-permute-start | bytes 104 | tf_op jit(solution)/shard_map/ppermute | solution.py:43
  7.5 0.4 collective-permute-start
  7.9 0.8 select_reduce_fusion.2
  8.7 0.7 pad_add_fusion
  9.5 0.6 reshape.154.facts_ref
  10.1 1.6 copy.46
  11.7 0.6 copy-done.12
  12.3 2.8 %shard_map.176 = (bf16[4,2,16,512]{3,2,1,0:T(8,128)(2,1)}, bf16[4,2,16,512]{3,2,1,0:T(8,128)(2,1)}, bf16[4,2,16,512]{3,2,1,0:T(8,128)(2,1)}, bf16[4,2,16,512]{3,2,1,0:T(8,128)(2,1)}) custom-call(s32[8]{0:T(128)} %get-tuple-element.38.refs_0_, s32[8]{0:T(128)} %copy-done.14, s32[8]{0:T(128)} %copy-done.13, s32[8]{0:T(128)} %copy-done.12, ...), custom_call_target="tpu_custom_call" | custom-call | bytes 1048576 | tf_op jit(solution)/shard_map/pallas_call | solution.py:105
  15.1 1.7 collective-permute-start.3
  16.8 0.9 collective-permute-start.5
  17.7 2.4 %collective-permute-start.6 = (bf16[4,2,16,512]{3,2,1,0:T(8,128)(2,1)}, bf16[4,2,16,512]{3,2,1,0:T(8,128)(2,1)S(1)}, u32[]{:S(2)}, u32[]{:S(2)}) collective-permute-start(bf16[4,2,16,512]{3,2,1,0:T(8,128)(2,1)} %get-tuple-element.50), channel_id=1, source_target_pairs={{0,64},{64,128},{128,192},{192,0},{1,65},{65,129},{129,193},{193,1... | collective-permute-start | bytes 393224 | tf_op jit(solution)/shard_map/ppermute | solution.py:43
  20.1 0.2 maximum_select_fusion
  20.3 4.1 %collective-permute-done.3.b1 = bf16[4,2,16,512]{3,2,1,0:T(8,128)(2,1)S(1)} collective-permute-done((bf16[4,2,16,512]{3,2,1,0:T(8,128)(2,1)}, bf16[4,2,16,512]{3,2,1,0:T(8,128)(2,1)S(1)}, u32[]{:S(2)}, u32[]{:S(2)}) %collective-permute-start.3) | collective-permute-done | bytes 131104 | tf_op jit(solution)/shard_map/ppermute | solution.py:43
  24.5 2.8 %collective-permute-start.9 = (bf16[256,512]{1,0:T(8,128)(2,1)S(1)}, bf16[256,512]{1,0:T(8,128)(2,1)S(1)}, u32[]{:S(2)}, u32[]{:S(2)}) collective-permute-start(bf16[256,512]{1,0:T(8,128)(2,1)S(1)} %get-tuple-element.78), channel_id=1, source_target_pairs={{0,6},{1,7},{2,0},{3,1},{4,2},{5,3},{6,4},{7,5},{8,14},{9,15},{10,... | collective-permute-start | bytes 786440 | tf_op jit(solution)/shard_map/ppermute | solution.py:51
  27.3 1.0 collective-permute-start.8
  28.2 0.8 collective-permute-start.7
  29.0 0.6 copy-done.7
  29.7 5.4 %shard_map.177 = bf16[64,1024]{1,0:T(8,128)(2,1)} custom-call(s32[56]{0:T(128)} %reshape.154.facts_ref, bf16[8,64,128]{2,1,0:T(8,128)(2,1)} %bitcast.62, bf16[8,512]{1,0:T(8,128)(2,1)} %key_ref.1, bf16[8,512]{1,0:T(8,128)(2,1)} %value_ref.1, bf16[8,2,64,512]{3,2,1,0:T(8,128)(2,1)} %resident_ref.1, bf16[4,2,16,512]{3,2,1,0:T(8,128)(2,1)} %get-tuple-element.47.b0, ...), custom_call_target="tpu_custom_call" | custom-call | flops 268435456 | bytes 3145728 | tf_op jit(solution)/shard_map/pallas_call | solution.py:177
  35.1 17.6 %all_to_all.20 = bf16[8,8,1024]{2,1,0:T(8,128)(2,1)S(1)} all-to-all(bf16[8,8,1024]{2,1,0:T(8,128)(2,1)} %bitcast.63), channel_id=1, replica_groups={{0,8,16,24,32,40,48,56},{1,9,17,25,33,41,49,57},{2,10,18,26,34,42,50,58..., dimensions={0} | all-to-all | bytes 262144 | tf_op jit(solution)/shard_map/all_to_all | solution.py:240
  52.8 2.5 %collective-permute-start.12 = (bf16[64,1024]{1,0:T(8,128)(2,1)S(1)}, bf16[64,1024]{1,0:T(8,128)(2,1)S(1)}, u32[]{:S(2)}, u32[]{:S(2)}) collective-permute-start(bf16[64,1024]{1,0:T(8,128)(2,1)S(1)} %bitcast.49), channel_id=1, source_target_pairs={{0,6},{1,7},{2,0},{3,1},{4,2},{5,3},{6,4},{7,5},{8,14},{9,15},{10,... | collective-permute-start | bytes 393224 | tf_op jit(solution)/shard_map/ppermute | solution.py:51
  55.3 1.7 collective-permute-start.11
  56.9 2.2 collective-permute-done.12.refs_3_
  59.2 2.5 %collective-permute-done.11.refs_2_ = bf16[64,1024]{1,0:T(8,128)(2,1)S(1)} collective-permute-done((bf16[64,1024]{1,0:T(8,128)(2,1)S(1)}, bf16[64,1024]{1,0:T(8,128)(2,1)S(1)}, u32[]{:S(2)}, u32[]{:S(2)}) %collective-permute-start.11) | collective-permute-done | bytes 131104 | tf_op jit(solution)/shard_map/ppermute | solution.py:51
  61.7 1.4 collective-permute-done.10.refs_1_
  63.4 1.8 collective-permute-done.13.other_ref
  65.2 1.3 shard_map.179
  66.4 0.8 copy-done.2
  67.2 5.9 %all-to-all-start.1 = ((bf16[64,8,512]{2,1,0:T(8,128)(2,1)}), bf16[64,8,512]{2,1,0:T(8,128)(2,1)}, u32[]{:S(2)}, u32[]{:S(2)}) async-start(bf16[64,8,512]{2,1,0:T(8,128)(2,1)} %bitcast.47), calls=%async_computation.1 | async-start | bytes 1048576 | tf_op jit(solution)/shard_map/all_to_all | solution.py:264
  73.8 1.2 select_convert_fusion
  75.0 1.4 convert_element_type.37.pick_ref
  76.3 14.3 %all-to-all-done.1 = bf16[64,8,512]{2,1,0:T(8,128)(2,1)} async-done(((bf16[64,8,512]{2,1,0:T(8,128)(2,1)}), bf16[64,8,512]{2,1,0:T(8,128)(2,1)}, u32[]{:S(2)}, u32[]{:S(2)}) %all-to-all-start.1) | async-done | bytes 524320 | tf_op jit(solution)/shard_map/all_to_all | solution.py:264
  90.7 1.8 shard_map.180
  92.5 34.5 %all_to_all.21 = bf16[64,8,1024]{2,1,0:T(8,128)(2,1)S(1)} all-to-all(bf16[64,8,1024]{2,1,0:T(8,128)(2,1)S(1)} %bitcast.48), channel_id=1, replica_groups=mesh['pool'=4,'ep'=64] {'ep'}, dimensions={0} | all-to-all | bytes 2097152 | tf_op jit(solution)/shard_map/all_to_all | solution.py:452
  126.9 3.2 %collective-permute-start.14 = (bf16[512,1024]{1,0:T(8,128)(2,1)S(1)}, bf16[512,1024]{1,0:T(8,128)(2,1)S(1)}, u32[]{:S(2)}, u32[]{:S(2)}) collective-permute-start(bf16[512,1024]{1,0:T(8,128)(2,1)S(1)} %bitcast.44), channel_id=1, source_target_pairs={{0,64},{64,128},{128,192},{192,0},{1,65},{65,129},{129,193},{193,1... | collective-permute-start | bytes 3145736 | tf_op jit(solution)/shard_map/ppermute | solution.py:43
  130.2 6.2 %shard_map.181 = bf16[512,1024]{1,0:T(8,128)(2,1)S(1)} custom-call(bf16[256,256]{1,0:T(8,128)(2,1)S(1)} %copy-done.3, bf16[512,1024]{1,0:T(8,128)(2,1)S(1)} %bitcast.45, bf16[4096,384]{1,0:T(8,128)(2,1)S(1)} %bitcast.41, bf16[4096,384]{1,0:T(8,128)(2,1)} %bitcast.53, bf16[384,4096]{1,0:T(8,128)(2,1)} %bitcast.56), custom_call_target="tpu_custom_call" | custom-call | flops 1207959552 | bytes 11534336 | tf_op jit(solution)/shard_map/pallas_call | solution.py:346
  136.3 16.0 %collective-permute-done.15.refs_1_ = bf16[512,1024]{1,0:T(8,128)(2,1)S(1)} collective-permute-done((bf16[512,1024]{1,0:T(8,128)(2,1)S(1)}, bf16[512,1024]{1,0:T(8,128)(2,1)S(1)}, u32[]{:S(2)}, u32[]{:S(2)}) %collective-permute-start.15) | collective-permute-done | bytes 1048608 | tf_op jit(solution)/shard_map/ppermute | solution.py:43
  152.4 3.0 %collective-permute-start.17 = (bf16[256,1024]{1,0:T(8,128)(2,1)S(1)}, bf16[256,1024]{1,0:T(8,128)(2,1)S(1)}, u32[]{:S(2)}, u32[]{:S(2)}) collective-permute-start(bf16[256,1024]{1,0:T(8,128)(2,1)S(1)} %slice.41), channel_id=1, source_target_pairs={{0,64},{64,128},{128,192},{192,0},{1,65},{65,129},{129,193},{193,1... | collective-permute-start | bytes 1572872 | tf_op jit(solution)/shard_map/ppermute | solution.py:43
  155.5 8.7 %shard_map.182 = (bf16[512,1024]{1,0:T(8,128)(2,1)S(1)}, bf16[512,1024]{1,0:T(8,128)(2,1)S(1)}) custom-call(bf16[256,256]{1,0:T(8,128)(2,1)S(1)} %copy-done.3, bf16[512,1024]{1,0:T(8,128)(2,1)S(1)} %collective-permute-done.14.refs_0_, bf16[512,1024]{1,0:T(8,128)(2,1)S(1)} %collective-permute-done.15.refs_1_, bf16[4096,384]{1,0:T(8,128)(2,1)} %bitcast.40, ...), custom_call_target="tpu_custom_call" | custom-call | flops 2415919104 | bytes 13631488 | tf_op jit(solution)/shard_map/pallas_call | solution.py:346
  164.2 3.3 %collective-permute-start.21 = (bf16[256,1024]{1,0:T(8,128)(2,1)S(1)}, bf16[256,1024]{1,0:T(8,128)(2,1)S(1)}, u32[]{:S(2)}, u32[]{:S(2)}) collective-permute-start(bf16[256,1024]{1,0:T(8,128)(2,1)S(1)} %slice.45), channel_id=1, source_target_pairs={{0,64},{64,128},{128,192},{192,0},{1,65},{65,129},{129,193},{193,1... | collective-permute-start | bytes 1572872 | tf_op jit(solution)/shard_map/ppermute | solution.py:43
  167.6 0.6 collective-permute-done.16.refs_0_
  168.2 6.2 %shard_map.183 = (bf16[256,1024]{1,0:T(8,128)(2,1)S(1)}, bf16[256,1024]{1,0:T(8,128)(2,1)S(1)}) custom-call(bf16[256,256]{1,0:T(8,128)(2,1)S(1)} %copy-done.3, bf16[256,1024]{1,0:T(8,128)(2,1)S(1)} %collective-permute-done.16.refs_0_, bf16[256,1024]{1,0:T(8,128)(2,1)S(1)} %collective-permute-done.17.refs_1_, bf16[4096,384]{1,0:T(8,128)(2,1)S(1)} %bitcast.42, ...), custom_call_target="tpu_custom_call" | custom-call | flops 1207959552 | bytes 11534336 | tf_op jit(solution)/shard_map/pallas_call | solution.py:346
  174.3 2.7 %collective-permute-start.18 = (bf16[256,1024]{1,0:T(8,128)(2,1)S(1)}, bf16[256,1024]{1,0:T(8,128)(2,1)S(1)}, u32[]{:S(2)}, u32[]{:S(2)}) collective-permute-start(bf16[256,1024]{1,0:T(8,128)(2,1)S(1)} %get-tuple-element.65), channel_id=1, source_target_pairs={{0,64},{64,128},{128,192},{192,0},{1,65},{65,129},{129,193},{193,1... | collective-permute-start | bytes 1572872 | tf_op jit(solution)/shard_map/ppermute | solution.py:43
  177.1 1.5 collective-permute-done.21
  178.5 3.4 %collective-permute-done.20 = bf16[256,1024]{1,0:T(8,128)(2,1)S(1)} collective-permute-done((bf16[256,1024]{1,0:T(8,128)(2,1)S(1)}, bf16[256,1024]{1,0:T(8,128)(2,1)S(1)}, u32[]{:S(2)}, u32[]{:S(2)}) %collective-permute-start.20) | collective-permute-done | bytes 524320 | tf_op jit(solution)/shard_map/ppermute | solution.py:43
  181.9 0.4 convert_add_fusion
  182.3 5.2 %collective-permute-done.18 = bf16[256,1024]{1,0:T(8,128)(2,1)S(1)} collective-permute-done((bf16[256,1024]{1,0:T(8,128)(2,1)S(1)}, bf16[256,1024]{1,0:T(8,128)(2,1)S(1)}, u32[]{:S(2)}, u32[]{:S(2)}) %collective-permute-start.18) | collective-permute-done | bytes 524320 | tf_op jit(solution)/shard_map/ppermute | solution.py:43
  187.5 3.4 %collective-permute-done.19 = bf16[256,1024]{1,0:T(8,128)(2,1)S(1)} collective-permute-done((bf16[256,1024]{1,0:T(8,128)(2,1)S(1)}, bf16[256,1024]{1,0:T(8,128)(2,1)S(1)}, u32[]{:S(2)}, u32[]{:S(2)}) %collective-permute-start.19) | collective-permute-done | bytes 524320 | tf_op jit(solution)/shard_map/ppermute | solution.py:43
  191.0 0.2 add_convert_fusion.1
  191.2 0.4 collective-permute-start.22
  191.5 0.2 add_convert_fusion
  191.7 1.8 collective-permute-start.23
  193.5 9.4 %collective-permute-done.22.right_ref = bf16[256,1024]{1,0:T(8,128)(2,1)S(1)} collective-permute-done((bf16[256,1024]{1,0:T(8,128)(2,1)S(1)}, bf16[256,1024]{1,0:T(8,128)(2,1)S(1)}, u32[]{:S(2)}, u32[]{:S(2)}) %collective-permute-start.22) | collective-permute-done | bytes 524320 | tf_op jit(solution)/shard_map/ppermute | solution.py:43
  203.0 1.5 collective-permute-done.23.left_ref
  204.5 1.2 shard_map.184
  205.6 7.3 %all-to-all-start.3 = ((bf16[64,8,1024]{2,1,0:T(8,128)(2,1)}), bf16[64,8,1024]{2,1,0:T(8,128)(2,1)S(1)}, u32[]{:S(2)}, u32[]{:S(2)}) async-start(bf16[64,8,1024]{2,1,0:T(8,128)(2,1)} %bitcast.25), calls=%async_computation.3 | async-start | bytes 2097152 | tf_op jit(solution)/shard_map/all_to_all | solution.py:452
  213.6 0.4 and_select_fusion
  214.0 0.5 select_n.156
  214.6 27.2 %all-to-all-done.3 = bf16[64,8,1024]{2,1,0:T(8,128)(2,1)S(1)} async-done(((bf16[64,8,1024]{2,1,0:T(8,128)(2,1)}), bf16[64,8,1024]{2,1,0:T(8,128)(2,1)S(1)}, u32[]{:S(2)}, u32[]{:S(2)}) %all-to-all-start.3) | async-done | bytes 1048608 | tf_op jit(solution)/shard_map/all_to_all | solution.py:452
  241.8 0.9 shard_map.185
  (76 shorter events, 2.3 us)
Async XLA Ops:
  1.9 18.2 %collective-permute-start.4 = (bf16[128,2048]{1,0:T(8,128)(2,1)S(1)}, bf16[128,2048]{1,0:T(8,128)(2,1)S(1)}, u32[]{:S(2)}, u32[]{:S(2)}) collective-permute-start(bf16[128,2048]{1,0:T(8,128)(2,1)S(1)} %get-tuple-element.83), channel_id=1, source_target_pairs={{0,1},{1,0},{2,3},{3,2},{4,5},{5,4},{6,7},{7,6},{8,9},{9,8},{10,11... | collective-permute-start | bytes 1572872 | tf_op jit(solution)/shard_map/ppermute | solution.py:51
  4.1 7.6 %collective-permute-start.2 = (s32[8]{0:T(128)S(1)}, s32[8]{0:T(128)S(1)}, u32[]{:S(2)}, u32[]{:S(2)}) collective-permute-start(s32[8]{0:T(128)S(1)} %get-tuple-element.87), channel_id=1, source_target_pairs={{0,192},{64,0},{128,64},{192,128},{1,193},{65,1},{129,65},{193,129... | collective-permute-start | bytes 104 | tf_op jit(solution)/shard_map/ppermute | solution.py:43
  4.8 6.9 %collective-permute-start.1 = (s32[8]{0:T(128)S(1)}, s32[8]{0:T(128)S(1)}, u32[]{:S(2)}, u32[]{:S(2)}) collective-permute-start(s32[8]{0:T(128)S(1)} %get-tuple-element.88), channel_id=1, source_target_pairs={{0,128},{64,192},{128,0},{192,64},{1,129},{65,193},{129,1},{193,65... | collective-permute-start | bytes 104 | tf_op jit(solution)/shard_map/ppermute | solution.py:43
  7.5 4.2 %collective-permute-start = (s32[8]{0:T(128)S(1)}, s32[8]{0:T(128)S(1)}, u32[]{:S(2)}, u32[]{:S(2)}) collective-permute-start(s32[8]{0:T(128)S(1)} %get-tuple-element.89), channel_id=1, source_target_pairs={{0,64},{64,128},{128,192},{192,0},{1,65},{65,129},{129,193},{193,1... | collective-permute-start | bytes 104 | tf_op jit(solution)/shard_map/ppermute | solution.py:43
  11.7 0.6 copy-start.12
  11.7 0.6 copy-start.13
  11.7 0.6 copy-start.14
  15.1 9.3 %collective-permute-start.3 = (bf16[4,2,16,512]{3,2,1,0:T(8,128)(2,1)}, bf16[4,2,16,512]{3,2,1,0:T(8,128)(2,1)S(1)}, u32[]{:S(2)}, u32[]{:S(2)}) collective-permute-start(bf16[4,2,16,512]{3,2,1,0:T(8,128)(2,1)} %get-tuple-element.42), channel_id=1, source_target_pairs={{0,192},{64,0},{128,64},{192,128},{1,193},{65,1},{129,65},{193,129... | collective-permute-start | bytes 393224 | tf_op jit(solution)/shard_map/ppermute | solution.py:43
  16.8 12.2 %collective-permute-start.5 = (bf16[4,2,16,512]{3,2,1,0:T(8,128)(2,1)}, bf16[4,2,16,512]{3,2,1,0:T(8,128)(2,1)S(1)}, u32[]{:S(2)}, u32[]{:S(2)}) collective-permute-start(bf16[4,2,16,512]{3,2,1,0:T(8,128)(2,1)} %get-tuple-element.49), channel_id=1, source_target_pairs={{0,128},{64,192},{128,0},{192,64},{1,129},{65,193},{129,1},{193,65... | collective-permute-start | bytes 393224 | tf_op jit(solution)/shard_map/ppermute | solution.py:43
  17.7 11.3 %collective-permute-start.6 = (bf16[4,2,16,512]{3,2,1,0:T(8,128)(2,1)}, bf16[4,2,16,512]{3,2,1,0:T(8,128)(2,1)S(1)}, u32[]{:S(2)}, u32[]{:S(2)}) collective-permute-start(bf16[4,2,16,512]{3,2,1,0:T(8,128)(2,1)} %get-tuple-element.50), channel_id=1, source_target_pairs={{0,64},{64,128},{128,192},{192,0},{1,65},{65,129},{129,193},{193,1... | collective-permute-start | bytes 393224 | tf_op jit(solution)/shard_map/ppermute | solution.py:43
  24.4 4.6 %copy-start.6 = (bf16[4,2,16,512]{3,2,1,0:T(8,128)(2,1)}, bf16[4,2,16,512]{3,2,1,0:T(8,128)(2,1)S(1)}, u32[]{:S(2)}) copy-start(bf16[4,2,16,512]{3,2,1,0:T(8,128)(2,1)S(1)} %collective-permute-done.3.b1) | copy-start | bytes 393220
  24.5 28.3 %collective-permute-start.9 = (bf16[256,512]{1,0:T(8,128)(2,1)S(1)}, bf16[256,512]{1,0:T(8,128)(2,1)S(1)}, u32[]{:S(2)}, u32[]{:S(2)}) collective-permute-start(bf16[256,512]{1,0:T(8,128)(2,1)S(1)} %get-tuple-element.78), channel_id=1, source_target_pairs={{0,6},{1,7},{2,0},{3,1},{4,2},{5,3},{6,4},{7,5},{8,14},{9,15},{10,... | collective-permute-start | bytes 786440 | tf_op jit(solution)/shard_map/ppermute | solution.py:51
  27.3 25.5 %collective-permute-start.8 = (bf16[256,512]{1,0:T(8,128)(2,1)S(1)}, bf16[256,512]{1,0:T(8,128)(2,1)S(1)}, u32[]{:S(2)}, u32[]{:S(2)}) collective-permute-start(bf16[256,512]{1,0:T(8,128)(2,1)S(1)} %get-tuple-element.79), channel_id=1, source_target_pairs={{0,4},{1,5},{2,6},{3,7},{4,0},{5,1},{6,2},{7,3},{8,12},{9,13},{10,... | collective-permute-start | bytes 786440 | tf_op jit(solution)/shard_map/ppermute | solution.py:51
  28.2 24.6 %collective-permute-start.7 = (bf16[256,512]{1,0:T(8,128)(2,1)S(1)}, bf16[256,512]{1,0:T(8,128)(2,1)S(1)}, u32[]{:S(2)}, u32[]{:S(2)}) collective-permute-start(bf16[256,512]{1,0:T(8,128)(2,1)S(1)} %get-tuple-element.80), channel_id=1, source_target_pairs={{0,2},{1,3},{2,4},{3,5},{4,6},{5,7},{6,0},{7,1},{8,10},{9,11},{10,... | collective-permute-start | bytes 786440 | tf_op jit(solution)/shard_map/ppermute | solution.py:51
  29.0 0.7 copy-start.7
  29.0 0.7 copy-start.8
  29.7 43.6 %copy-start.9 = (s32[8,8]{1,0:T(8,128)S(1)}, s32[8,8]{1,0:T(8,128)}, u32[]{:S(2)}) copy-start(s32[8,8]{1,0:T(8,128)} %param.28) | copy-start | bytes 772
  29.7 43.8 %copy-start.11 = (bf16[4096]{0:T(1024)(128)(2,1)S(1)}, bf16[4096]{0:T(1024)(128)(2,1)}, u32[]{:S(2)}) copy-start(bf16[4096]{0:T(1024)(128)(2,1)} %param.27) | copy-start | bytes 24580
  35.1 55.6 %copy-start.4 = (bf16[8,4096]{1,0:T(8,128)(2,1)S(1)}, bf16[8,4096]{1,0:T(8,128)(2,1)}, u32[]{:S(2)}) copy-start(bf16[8,4096]{1,0:T(8,128)(2,1)} %residual_ref.1) | copy-start | bytes 196612
  52.8 6.4 %collective-permute-start.12 = (bf16[64,1024]{1,0:T(8,128)(2,1)S(1)}, bf16[64,1024]{1,0:T(8,128)(2,1)S(1)}, u32[]{:S(2)}, u32[]{:S(2)}) collective-permute-start(bf16[64,1024]{1,0:T(8,128)(2,1)S(1)} %bitcast.49), channel_id=1, source_target_pairs={{0,6},{1,7},{2,0},{3,1},{4,2},{5,3},{6,4},{7,5},{8,14},{9,15},{10,... | collective-permute-start | bytes 393224 | tf_op jit(solution)/shard_map/ppermute | solution.py:51
  55.3 6.5 %collective-permute-start.11 = (bf16[64,1024]{1,0:T(8,128)(2,1)S(1)}, bf16[64,1024]{1,0:T(8,128)(2,1)S(1)}, u32[]{:S(2)}, u32[]{:S(2)}) collective-permute-start(bf16[64,1024]{1,0:T(8,128)(2,1)S(1)} %bitcast.50), channel_id=1, source_target_pairs={{0,4},{1,5},{2,6},{3,7},{4,0},{5,1},{6,2},{7,3},{8,12},{9,13},{10,... | collective-permute-start | bytes 393224 | tf_op jit(solution)/shard_map/ppermute | solution.py:51
  56.9 6.2 %collective-permute-start.10 = (bf16[64,1024]{1,0:T(8,128)(2,1)S(1)}, bf16[64,1024]{1,0:T(8,128)(2,1)S(1)}, u32[]{:S(2)}, u32[]{:S(2)}) collective-permute-start(bf16[64,1024]{1,0:T(8,128)(2,1)S(1)} %bitcast.51), channel_id=1, source_target_pairs={{0,2},{1,3},{2,4},{3,5},{4,6},{5,7},{6,0},{7,1},{8,10},{9,11},{10,... | collective-permute-start | bytes 393224 | tf_op jit(solution)/shard_map/ppermute | solution.py:51
  63.2 2.0 collective-permute-start.13
  66.4 0.8 copy-start.2
  67.2 62.9 %copy-start = (bf16[1,4096,384]{2,1,0:T(8,128)(2,1)S(1)}, bf16[1,4096,384]{2,1,0:T(8,128)(2,1)}, u32[]{:S(2)}) copy-start(bf16[1,4096,384]{2,1,0:T(8,128)(2,1)} %param.30) | copy-start | bytes 9437188
  67.2 62.9 %copy-start.3 = (bf16[256,256]{1,0:T(8,128)(2,1)S(1)}, bf16[256,256]{1,0:T(8,128)(2,1)}, u32[]{:S(2)}) copy-start(bf16[256,256]{1,0:T(8,128)(2,1)} %constant.113.clone.order_ref) | copy-start | bytes 393220
  67.2 23.4 %all-to-all-start.1 = ((bf16[64,8,512]{2,1,0:T(8,128)(2,1)}), bf16[64,8,512]{2,1,0:T(8,128)(2,1)}, u32[]{:S(2)}, u32[]{:S(2)}) async-start(bf16[64,8,512]{2,1,0:T(8,128)(2,1)} %bitcast.47), calls=%async_computation.1 | async-start | bytes 1048576 | tf_op jit(solution)/shard_map/all_to_all | solution.py:264
  126.9 25.4 %collective-permute-start.15 = (bf16[512,1024]{1,0:T(8,128)(2,1)S(1)}, bf16[512,1024]{1,0:T(8,128)(2,1)S(1)}, u32[]{:S(2)}, u32[]{:S(2)}) collective-permute-start(bf16[512,1024]{1,0:T(8,128)(2,1)S(1)} %bitcast.43), channel_id=1, source_target_pairs={{0,192},{64,0},{128,64},{192,128},{1,193},{65,1},{129,65},{193,129... | collective-permute-start | bytes 3145736 | tf_op jit(solution)/shard_map/ppermute | solution.py:43
  126.9 25.4 %collective-permute-start.14 = (bf16[512,1024]{1,0:T(8,128)(2,1)S(1)}, bf16[512,1024]{1,0:T(8,128)(2,1)S(1)}, u32[]{:S(2)}, u32[]{:S(2)}) collective-permute-start(bf16[512,1024]{1,0:T(8,128)(2,1)S(1)} %bitcast.44), channel_id=1, source_target_pairs={{0,64},{64,128},{128,192},{192,0},{1,65},{65,129},{129,193},{193,1... | collective-permute-start | bytes 3145736 | tf_op jit(solution)/shard_map/ppermute | solution.py:43
  152.4 15.1 %collective-permute-start.17 = (bf16[256,1024]{1,0:T(8,128)(2,1)S(1)}, bf16[256,1024]{1,0:T(8,128)(2,1)S(1)}, u32[]{:S(2)}, u32[]{:S(2)}) collective-permute-start(bf16[256,1024]{1,0:T(8,128)(2,1)S(1)} %slice.41), channel_id=1, source_target_pairs={{0,64},{64,128},{128,192},{192,0},{1,65},{65,129},{129,193},{193,1... | collective-permute-start | bytes 1572872 | tf_op jit(solution)/shard_map/ppermute | solution.py:43
  155.5 12.7 %collective-permute-start.16 = (bf16[256,1024]{1,0:T(8,128)(2,1)S(1)}, bf16[256,1024]{1,0:T(8,128)(2,1)S(1)}, u32[]{:S(2)}, u32[]{:S(2)}) collective-permute-start(bf16[256,1024]{1,0:T(8,128)(2,1)S(1)} %slice.40), channel_id=1, source_target_pairs={{0,192},{64,0},{128,64},{192,128},{1,193},{65,1},{129,65},{193,129... | collective-permute-start | bytes 1572872 | tf_op jit(solution)/shard_map/ppermute | solution.py:43
  155.5 12.7 %copy-start.1 = (bf16[1,4096,384]{2,1,0:T(8,128)(2,1)S(1)}, bf16[1,4096,384]{2,1,0:T(8,128)(2,1)}, u32[]{:S(2)}) copy-start(bf16[1,4096,384]{2,1,0:T(8,128)(2,1)} %param.30) | copy-start | bytes 9437188
  164.2 14.3 %collective-permute-start.21 = (bf16[256,1024]{1,0:T(8,128)(2,1)S(1)}, bf16[256,1024]{1,0:T(8,128)(2,1)S(1)}, u32[]{:S(2)}, u32[]{:S(2)}) collective-permute-start(bf16[256,1024]{1,0:T(8,128)(2,1)S(1)} %slice.45), channel_id=1, source_target_pairs={{0,64},{64,128},{128,192},{192,0},{1,65},{65,129},{129,193},{193,1... | collective-permute-start | bytes 1572872 | tf_op jit(solution)/shard_map/ppermute | solution.py:43
  167.6 14.4 %collective-permute-start.20 = (bf16[256,1024]{1,0:T(8,128)(2,1)S(1)}, bf16[256,1024]{1,0:T(8,128)(2,1)S(1)}, u32[]{:S(2)}, u32[]{:S(2)}) collective-permute-start(bf16[256,1024]{1,0:T(8,128)(2,1)S(1)} %slice.43), channel_id=1, source_target_pairs={{0,192},{64,0},{128,64},{192,128},{1,193},{65,1},{129,65},{193,129... | collective-permute-start | bytes 1572872 | tf_op jit(solution)/shard_map/ppermute | solution.py:43
  174.3 13.2 %collective-permute-start.18 = (bf16[256,1024]{1,0:T(8,128)(2,1)S(1)}, bf16[256,1024]{1,0:T(8,128)(2,1)S(1)}, u32[]{:S(2)}, u32[]{:S(2)}) collective-permute-start(bf16[256,1024]{1,0:T(8,128)(2,1)S(1)} %get-tuple-element.65), channel_id=1, source_target_pairs={{0,64},{64,128},{128,192},{192,0},{1,65},{65,129},{129,193},{193,1... | collective-permute-start | bytes 1572872 | tf_op jit(solution)/shard_map/ppermute | solution.py:43
  177.1 13.9 %collective-permute-start.19 = (bf16[256,1024]{1,0:T(8,128)(2,1)S(1)}, bf16[256,1024]{1,0:T(8,128)(2,1)S(1)}, u32[]{:S(2)}, u32[]{:S(2)}) collective-permute-start(bf16[256,1024]{1,0:T(8,128)(2,1)S(1)} %get-tuple-element.66), channel_id=1, source_target_pairs={{0,192},{64,0},{128,64},{192,128},{1,193},{65,1},{129,65},{193,129... | collective-permute-start | bytes 1572872 | tf_op jit(solution)/shard_map/ppermute | solution.py:43
  191.2 11.8 %collective-permute-start.22 = (bf16[256,1024]{1,0:T(8,128)(2,1)S(1)}, bf16[256,1024]{1,0:T(8,128)(2,1)S(1)}, u32[]{:S(2)}, u32[]{:S(2)}) collective-permute-start(bf16[256,1024]{1,0:T(8,128)(2,1)S(1)} %add_convert_fusion.1), channel_id=1, source_target_pairs={{0,64},{64,128},{128,192},{192,0},{1,65},{65,129},{129,193},{193,1... | collective-permute-start | bytes 1572872 | tf_op jit(solution)/shard_map/ppermute | solution.py:43
  191.7 21.4 %copy-start.10 = (f32[8,8]{1,0:T(8,128)S(1)}, f32[8,8]{1,0:T(8,128)}, u32[]{:S(2)}) copy-start(f32[8,8]{1,0:T(8,128)} %param.29) | copy-start | bytes 772
  191.7 12.7 %collective-permute-start.23 = (bf16[256,1024]{1,0:T(8,128)(2,1)S(1)}, bf16[256,1024]{1,0:T(8,128)(2,1)S(1)}, u32[]{:S(2)}, u32[]{:S(2)}) collective-permute-start(bf16[256,1024]{1,0:T(8,128)(2,1)S(1)} %add_convert_fusion), channel_id=1, source_target_pairs={{0,192},{64,0},{128,64},{192,128},{1,193},{65,1},{129,65},{193,129... | collective-permute-start | bytes 1572872 | tf_op jit(solution)/shard_map/ppermute | solution.py:43
  205.6 36.2 %copy-start.5 = (bf16[8,4096]{1,0:T(8,128)(2,1)S(1)}, bf16[8,4096]{1,0:T(8,128)(2,1)}, u32[]{:S(2)}) copy-start(bf16[8,4096]{1,0:T(8,128)(2,1)} %get-tuple-element.36.attended_ref) | copy-start | bytes 196612
  205.6 36.2 %all-to-all-start.3 = ((bf16[64,8,1024]{2,1,0:T(8,128)(2,1)}), bf16[64,8,1024]{2,1,0:T(8,128)(2,1)S(1)}, u32[]{:S(2)}, u32[]{:S(2)}) async-start(bf16[64,8,1024]{2,1,0:T(8,128)(2,1)} %bitcast.25), calls=%async_computation.3 | async-start | bytes 2097152 | tf_op jit(solution)/shard_map/all_to_all | solution.py:452
where the time goes:
time: 244 us; the launch traced here: 243 us
  waiting for transfers between devices  94.7 us (39%)
  blocking collectives  52.1 us (21%)
  starting transfers between devices  45.4 us (19%)
  Pallas kernels  34.4 us (14%)
  local copies, waits for them, and re-layouts  8.9 us (4%)
  other arithmetic  6.22 us (3%)
    ppermute x16, waiting for transfers between devices, shift_pool(): lax.ppermute(value, 'pool', [(i, (i + step) % N_POOL) for i in range(N_PO...  45.1 us
    all_to_all x1, blocking collectives, exchange(): lax.all_to_all(parted, 'ep', split_axis=0, concat_axis=0, tiled=True)  34.5 us
    all_to_all x1, waiting for transfers between devices, exchange(): lax.all_to_all(parted, 'ep', split_axis=0, concat_axis=0, tiled=True)  27.2 us
    ppermute x16, starting transfers between devices, shift_pool(): lax.ppermute(value, 'pool', [(i, (i + step) % N_POOL) for i in range(N_PO...  23.4 us
    pallas_call x3, Pallas kernels, expert(): pl.pallas_call(functools.partial(expert_kernel, layout), grid=(2 * STEPS,...  21 us
    all_to_all x1, blocking collectives, project(): lax.all_to_all(context.reshape(N_Z, ROWS, DEEP), 'ep', split_axis=0, conc...  17.6 us
    all_to_all x1, waiting for transfers between devices, project(): lax.all_to_all(product.reshape(N_EP, ROWS, CHUNK), 'ep', split_axis=0, co...  14.3 us
    ppermute x8, starting transfers between devices, shift_ep(): return lax.ppermute(value, 'ep', pairs)  8.84 us
  transfers between devices with their start and end apart: 26, of which 15 were waited for; matrix products, arithmetic and copies ran while one was open for 5% of the time, Pallas kernels for 12%

commit v1 on v0

--- a/solution.py
+++ b/solution.py
@@ -363,9 +363,9 @@
     )(order, *arrays, w_gate, w_up, w_down)
 
 
-def sum_kernel(base_a_ref, base_b_ref, right_ref, left_ref, out_ref):
-    out_ref[:HALF, :] = (base_a_ref[...] + right_ref[...].astype(jnp.float32)).astype(jnp.bfloat16)
-    out_ref[HALF:, :] = (base_b_ref[...] + left_ref[...].astype(jnp.float32)).astype(jnp.bfloat16)
+def sum_kernel(base_a_ref, base_b_ref, more_a_ref, more_b_ref, out_ref):
+    out_ref[:HALF, :] = (base_a_ref[...] + more_a_ref[...].astype(jnp.float32)).astype(jnp.bfloat16)
+    out_ref[HALF:, :] = (base_b_ref[...] + more_b_ref[...].astype(jnp.float32)).astype(jnp.bfloat16)
 
 
 def finish_kernel(mix_ref, returned_ref, attended_ref, out_ref):
@@ -453,28 +453,31 @@
 
     weights = (expert_gate[0], expert_up[0], expert_down[0], jnp.asarray(order_matrix()))
     mine = exchange(outgoing)
-    left, right = shift_pool(mine, 1), shift_pool(mine, -1)
+    tie = lax.optimization_barrier
+    low, high = mine[:HALF], mine[HALF:]
+    right_a, left_b = shift_pool(low, -1), shift_pool(high, 1)
+    left_a, right_b = shift_pool(low, 1), shift_pool(high, -1)
     (own,) = expert([mine], *weights)
-    left, right, own = lax.optimization_barrier((left, right, own))
-    far_a, far_b = shift_pool(right[:HALF], -1), shift_pool(left[HALF:], 1)
-    to_left, to_right = expert([left, right], *weights)
-    right_b, left_a = shift_pool(to_right[HALF:], 1), shift_pool(to_left[:HALF], -1)
-    far_a, far_b, to_left, to_right = lax.optimization_barrier((far_a, far_b, to_left, to_right))
+    right_a, left_b, own = tie((right_a, left_b, own))
+    far_a, far_b = shift_pool(right_a, -1), shift_pool(left_b, 1)
+    to_left_a, to_left_b, to_right_a, to_right_b = expert([left_a, left_b, right_a, right_b], *weights)
+    from_left_b, from_right_a = shift_pool(to_right_b, 1), shift_pool(to_left_a, -1)
+    far_a, far_b, to_left_b, to_right_a = tie((far_a, far_b, to_left_b, to_right_a))
     to_far_a, to_far_b = expert([far_a, far_b], *weights)
     over_a, over_b = shift_pool(to_far_a, 1), shift_pool(to_far_b, -1)
 
     def wide(value):
         return value.astype(jnp.float32)
 
-    base_a, base_b = wide(own[:HALF]) + wide(left_a), wide(own[HALF:]) + wide(right_b)
-    over_a, over_b, base_a, base_b = lax.optimization_barrier((over_a, over_b, base_a, base_b))
-    right_a = shift_pool((wide(to_right[:HALF]) + wide(over_a)).astype(jnp.bfloat16), 1)
-    left_b = shift_pool((wide(to_left[HALF:]) + wide(over_b)).astype(jnp.bfloat16), -1)
+    base_a, base_b = wide(own[:HALF]) + wide(from_right_a), wide(own[HALF:]) + wide(from_left_b)
+    over_a, over_b, base_a, base_b = tie((over_a, over_b, base_a, base_b))
+    from_left_a = shift_pool((wide(to_right_a) + wide(over_a)).astype(jnp.bfloat16), 1)
+    from_right_b = shift_pool((wide(to_left_b) + wide(over_b)).astype(jnp.bfloat16), -1)
     summed = pl.pallas_call(
         sum_kernel,
         out_shape=jax.ShapeDtypeStruct(message, jnp.bfloat16),
         compiler_params=pltpu.CompilerParams(vmem_limit_bytes=BIG),
-    )(base_a, base_b, right_a, left_b)
+    )(base_a, base_b, from_left_a, from_right_b)
     returned = exchange(summed)
     layer_out = pl.pallas_call(
         finish_kernel,

time: 244 us -> 239 us (0.980); the launches traced: 243 us -> 235 us
  waiting for transfers between devices: 94.7 us -> 83.8 us
  starting transfers between devices: 45.4 us -> 48.7 us
    ppermute x16 -> x18, waiting for transfers between devices: 45.1 us -> 35.2 us  [shift_pool(): lax.ppermute(value, 'pool', [(i, (i + step) % N_POOL) for i in range(N_PO...]
    ppermute x16 -> x18, starting transfers between devices: 23.4 us -> 25.4 us  [shift_pool(): lax.ppermute(value, 'pool', [(i, (i + step) % N_POOL) for i in range(N_PO...]
  transfers between devices with their start and end apart: 26 -> 28, of which waited for: 15 -> 16; matrix products, arithmetic and copies ran while one was open for 5% -> 5% of each run, Pallas kernels for 12% -> 12%
where the time goes in v1:
time: 239 us; the launch traced here: 235 us
  waiting for transfers between devices  83.8 us (35%)
  blocking collectives  52.2 us (22%)
  starting transfers between devices  48.7 us (20%)
  Pallas kernels  34.9 us (15%)
  local copies, waits for them, and re-layouts  7.93 us (3%)
  other arithmetic  6.23 us (3%)
    ppermute x18, waiting for transfers between devices, shift_pool(): lax.ppermute(value, 'pool', [(i, (i + step) % N_POOL) for i in range(N_PO...  35.2 us
    all_to_all x1, blocking collectives, exchange(): lax.all_to_all(parted, 'ep', split_axis=0, concat_axis=0, tiled=True)  34.5 us
    all_to_all x1, waiting for transfers between devices, exchange(): lax.all_to_all(parted, 'ep', split_axis=0, concat_axis=0, tiled=True)  27.2 us
    ppermute x18, starting transfers between devices, shift_pool(): lax.ppermute(value, 'pool', [(i, (i + step) % N_POOL) for i in range(N_PO...  25.4 us
    pallas_call x3, Pallas kernels, expert(): pl.pallas_call(functools.partial(expert_kernel, layout), grid=(2 * STEPS,...  20.9 us
    all_to_all x1, blocking collectives, project(): lax.all_to_all(context.reshape(N_Z, ROWS, DEEP), 'ep', split_axis=0, conc...  17.7 us
    all_to_all x1, waiting for transfers between devices, project(): lax.all_to_all(product.reshape(N_EP, ROWS, CHUNK), 'ep', split_axis=0, co...  14.3 us
    ppermute x8, starting transfers between devices, shift_ep(): return lax.ppermute(value, 'ep', pairs)  9.75 us
  transfers between devices with their start and end apart: 28, of which 16 were waited for; matrix products, arithmetic and copies ran while one was open for 5% of the time, Pallas kernels for 12%

profile of v1, /device:TPU:24, one launch (start us, length us, event | category | flops | bytes accessed | tf_op | source)
XLA Modules:
  0.0 234.7 jit_solution(1794773022789260181)
XLA Ops:
  0.7 1.3 dynamic-slice_bitcast_fusion
  2.0 0.7 add_select_fusion
  2.7 0.7 broadcast_compare_fusion.1
  3.6 0.5 slice_bitcast_fusion.2
  4.1 2.0 collective-permute-start
  6.0 0.9 collective-permute-start.1
  6.9 0.8 select_reduce_fusion.2
  7.7 0.7 pad_add_fusion
  8.4 0.6 reshape.156.facts_ref
  9.0 1.6 copy.46
  10.6 0.5 collective-permute-done.1.refs_2_
  11.1 0.6 collective-permute-done.2.refs_3_
  11.6 0.5 copy-done.13
  12.2 2.7 %shard_map.176 = (bf16[4,2,16,512]{3,2,1,0:T(8,128)(2,1)}, bf16[4,2,16,512]{3,2,1,0:T(8,128)(2,1)}, bf16[4,2,16,512]{3,2,1,0:T(8,128)(2,1)}, bf16[4,2,16,512]{3,2,1,0:T(8,128)(2,1)}) custom-call(s32[8]{0:T(128)} %get-tuple-element.40.refs_0_, s32[8]{0:T(128)} %copy-done.11, s32[8]{0:T(128)} %copy-done.12, s32[8]{0:T(128)} %copy-done.13, ...), custom_call_target="tpu_custom_call" | custom-call | bytes 1048576 | tf_op jit(solution)/shard_map/pallas_call | solution.py:105
  14.8 1.8 collective-permute-start.3
  16.6 2.1 collective-permute-start.5
  18.7 1.2 collective-permute-start.6
  20.1 1.8 collective-permute-done.3.b1
  22.0 1.5 collective-permute-start.7
  23.6 2.6 %collective-permute-start.8 = (bf16[256,512]{1,0:T(8,128)(2,1)S(1)}, bf16[256,512]{1,0:T(8,128)(2,1)S(1)}, u32[]{:S(2)}, u32[]{:S(2)}) collective-permute-start(bf16[256,512]{1,0:T(8,128)(2,1)S(1)} %get-tuple-element.85), channel_id=1, source_target_pairs={{0,4},{1,5},{2,6},{3,7},{4,0},{5,1},{6,2},{7,3},{8,12},{9,13},{10,... | collective-permute-start | bytes 786440 | tf_op jit(solution)/shard_map/ppermute | solution.py:51
  26.1 2.2 collective-permute-start.9
  28.3 0.6 copy-done.6
  29.0 5.4 %shard_map.177 = bf16[64,1024]{1,0:T(8,128)(2,1)} custom-call(s32[56]{0:T(128)} %reshape.156.facts_ref, bf16[8,64,128]{2,1,0:T(8,128)(2,1)} %bitcast.63, bf16[8,512]{1,0:T(8,128)(2,1)} %key_ref.1, bf16[8,512]{1,0:T(8,128)(2,1)} %value_ref.1, bf16[8,2,64,512]{3,2,1,0:T(8,128)(2,1)} %resident_ref.1, bf16[4,2,16,512]{3,2,1,0:T(8,128)(2,1)} %get-tuple-element.49.b0, ...), custom_call_target="tpu_custom_call" | custom-call | flops 268435456 | bytes 3145728 | tf_op jit(solution)/shard_map/pallas_call | solution.py:177
  34.4 17.7 %all_to_all.20 = bf16[8,8,1024]{2,1,0:T(8,128)(2,1)S(1)} all-to-all(bf16[8,8,1024]{2,1,0:T(8,128)(2,1)} %bitcast.64), channel_id=1, replica_groups={{0,8,16,24,32,40,48,56},{1,9,17,25,33,41,49,57},{2,10,18,26,34,42,50,58..., dimensions={0} | all-to-all | bytes 262144 | tf_op jit(solution)/shard_map/all_to_all | solution.py:240
  52.2 0.3 collective-permute-start.10
  52.5 1.2 collective-permute-start.11
  53.7 1.8 collective-permute-start.12
  55.5 4.3 %collective-permute-done.10.refs_1_ = bf16[64,1024]{1,0:T(8,128)(2,1)S(1)} collective-permute-done((bf16[64,1024]{1,0:T(8,128)(2,1)S(1)}, bf16[64,1024]{1,0:T(8,128)(2,1)S(1)}, u32[]{:S(2)}, u32[]{:S(2)}) %collective-permute-start.10) | collective-permute-done | bytes 131104 | tf_op jit(solution)/shard_map/ppermute | solution.py:51
  59.8 0.9 collective-permute-done.12.refs_3_
  61.0 1.8 collective-permute-done.13.other_ref
  62.8 2.1 shard_map.179
  64.8 5.7 %all-to-all-start.1 = ((bf16[64,8,512]{2,1,0:T(8,128)(2,1)}), bf16[64,8,512]{2,1,0:T(8,128)(2,1)}, u32[]{:S(2)}, u32[]{:S(2)}) async-start(bf16[64,8,512]{2,1,0:T(8,128)(2,1)} %bitcast.16), calls=%async_computation.1 | async-start | bytes 1048576 | tf_op jit(solution)/shard_map/all_to_all | solution.py:264
  71.1 1.2 select_convert_fusion
  72.3 1.4 convert_element_type.37.pick_ref
  73.7 14.3 %all-to-all-done.1 = bf16[64,8,512]{2,1,0:T(8,128)(2,1)} async-done(((bf16[64,8,512]{2,1,0:T(8,128)(2,1)}), bf16[64,8,512]{2,1,0:T(8,128)(2,1)}, u32[]{:S(2)}, u32[]{:S(2)}) %all-to-all-start.1) | async-done | bytes 524320 | tf_op jit(solution)/shard_map/all_to_all | solution.py:264
  88.0 1.8 shard_map.180
  89.8 34.5 %all_to_all.21 = bf16[64,8,1024]{2,1,0:T(8,128)(2,1)S(1)} all-to-all(bf16[64,8,1024]{2,1,0:T(8,128)(2,1)S(1)} %bitcast.49), channel_id=1, replica_groups=mesh['pool'=4,'ep'=64] {'ep'}, dimensions={0} | all-to-all | bytes 2097152 | tf_op jit(solution)/shard_map/all_to_all | solution.py:452
  124.4 3.2 %collective-permute-start.15 = (bf16[256,1024]{1,0:T(8,128)(2,1)S(1)}, bf16[256,1024]{1,0:T(8,128)(2,1)S(1)}, u32[]{:S(2)}, u32[]{:S(2)}) collective-permute-start(bf16[256,1024]{1,0:T(8,128)(2,1)S(1)} %get-tuple-element.82), channel_id=1, source_target_pairs={{0,64},{64,128},{128,192},{192,0},{1,65},{65,129},{129,193},{193,1... | collective-permute-start | bytes 1572872 | tf_op jit(solution)/shard_map/ppermute | solution.py:43
  127.7 1.9 collective-permute-start.19
  129.7 6.1 %shard_map.181 = bf16[512,1024]{1,0:T(8,128)(2,1)S(1)} custom-call(bf16[256,256]{1,0:T(8,128)(2,1)S(1)} %copy-done.2, bf16[512,1024]{1,0:T(8,128)(2,1)S(1)} %bitcast.47, bf16[4096,384]{1,0:T(8,128)(2,1)S(1)} %bitcast.45, bf16[4096,384]{1,0:T(8,128)(2,1)} %bitcast.54, bf16[384,4096]{1,0:T(8,128)(2,1)} %bitcast.57), custom_call_target="tpu_custom_call" | custom-call | flops 1207959552 | bytes 11534336 | tf_op jit(solution)/shard_map/pallas_call | solution.py:346
  135.8 4.6 %collective-permute-done.14.refs_2_ = bf16[256,1024]{1,0:T(8,128)(2,1)S(1)} collective-permute-done((bf16[256,1024]{1,0:T(8,128)(2,1)S(1)}, bf16[256,1024]{1,0:T(8,128)(2,1)S(1)}, u32[]{:S(2)}, u32[]{:S(2)}) %collective-permute-start.14) | collective-permute-done | bytes 524320 | tf_op jit(solution)/shard_map/ppermute | solution.py:43
  140.6 3.1 %collective-permute-start.17 = (bf16[256,1024]{1,0:T(8,128)(2,1)S(1)}, bf16[256,1024]{1,0:T(8,128)(2,1)S(1)}, u32[]{:S(2)}, u32[]{:S(2)}) collective-permute-start(bf16[256,1024]{1,0:T(8,128)(2,1)S(1)} %collective-permute-done.15.refs_1_), channel_id=1, source_target_pairs={{0,64},{64,128},{128,192},{192,0},{1,65},{65,129},{129,193},{193,1... | collective-permute-start | bytes 1572872 | tf_op jit(solution)/shard_map/ppermute | solution.py:43
  143.7 7.5 %collective-permute-done.18.refs_0_ = bf16[256,1024]{1,0:T(8,128)(2,1)S(1)} collective-permute-done((bf16[256,1024]{1,0:T(8,128)(2,1)S(1)}, bf16[256,1024]{1,0:T(8,128)(2,1)S(1)}, u32[]{:S(2)}, u32[]{:S(2)}) %collective-permute-start.18) | collective-permute-done | bytes 524320 | tf_op jit(solution)/shard_map/ppermute | solution.py:43
  151.3 0.5 collective-permute-done.19.refs_3_
  151.7 8.5 %shard_map.182 = (bf16[256,1024]{1,0:T(8,128)(2,1)S(1)}, bf16[256,1024]{1,0:T(8,128)(2,1)S(1)}, bf16[256,1024]{1,0:T(8,128)(2,1)S(1)}, bf16[256,1024]{1,0:T(8,128)(2,1)S(1)}) custom-call(bf16[256,256]{1,0:T(8,128)(2,1)S(1)} %copy-done.2, bf16[256,1024]{1,0:T(8,128)(2,1)S(1)} %collective-permute-done.18.refs_0_, ...), custom_call_target="tpu_custom_call" | custom-call | flops 2415919104 | bytes 13631488 | tf_op jit(solution)/shard_map/pallas_call | solution.py:346
  160.2 0.2 collective-permute-start.22
  160.5 3.2 %collective-permute-start.23 = (bf16[256,1024]{1,0:T(8,128)(2,1)S(1)}, bf16[256,1024]{1,0:T(8,128)(2,1)S(1)}, u32[]{:S(2)}, u32[]{:S(2)}) collective-permute-start(bf16[256,1024]{1,0:T(8,128)(2,1)S(1)} %get-tuple-element.71), channel_id=1, source_target_pairs={{0,64},{64,128},{128,192},{192,0},{1,65},{65,129},{129,193},{193,1... | collective-permute-start | bytes 1572872 | tf_op jit(solution)/shard_map/ppermute | solution.py:43
  163.7 6.2 %shard_map.183 = (bf16[256,1024]{1,0:T(8,128)(2,1)S(1)}, bf16[256,1024]{1,0:T(8,128)(2,1)S(1)}) custom-call(bf16[256,256]{1,0:T(8,128)(2,1)S(1)} %copy-done.2, bf16[256,1024]{1,0:T(8,128)(2,1)S(1)} %collective-permute-done.16.refs_0_, bf16[256,1024]{1,0:T(8,128)(2,1)S(1)} %collective-permute-done.17.refs_1_, bf16[4096,384]{1,0:T(8,128)(2,1)S(1)} %bitcast.46, ...), custom_call_target="tpu_custom_call" | custom-call | flops 1207959552 | bytes 11534336 | tf_op jit(solution)/shard_map/pallas_call | solution.py:346
  169.8 2.0 collective-permute-start.20
  172.0 0.8 collective-permute-done.22
  172.8 1.9 collective-permute-done.23
  174.7 0.4 convert_add_fusion
  175.1 7.7 %collective-permute-done.20 = bf16[256,1024]{1,0:T(8,128)(2,1)S(1)} collective-permute-done((bf16[256,1024]{1,0:T(8,128)(2,1)S(1)}, bf16[256,1024]{1,0:T(8,128)(2,1)S(1)}, u32[]{:S(2)}, u32[]{:S(2)}) %collective-permute-start.20) | collective-permute-done | bytes 524320 | tf_op jit(solution)/shard_map/ppermute | solution.py:43
  182.8 0.7 collective-permute-done.21
  183.5 0.2 add_convert_fusion
  183.7 0.4 collective-permute-start.25
  184.3 3.0 %collective-permute-start.24 = (bf16[256,1024]{1,0:T(8,128)(2,1)S(1)}, bf16[256,1024]{1,0:T(8,128)(2,1)S(1)}, u32[]{:S(2)}, u32[]{:S(2)}) collective-permute-start(bf16[256,1024]{1,0:T(8,128)(2,1)S(1)} %add_convert_fusion.1), channel_id=1, source_target_pairs={{0,64},{64,128},{128,192},{192,0},{1,65},{65,129},{129,193},{193,1... | collective-permute-start | bytes 1572872 | tf_op jit(solution)/shard_map/ppermute | solution.py:43
  187.3 8.5 %collective-permute-done.25.more_b_ref = bf16[256,1024]{1,0:T(8,128)(2,1)S(1)} collective-permute-done((bf16[256,1024]{1,0:T(8,128)(2,1)S(1)}, bf16[256,1024]{1,0:T(8,128)(2,1)S(1)}, u32[]{:S(2)}, u32[]{:S(2)}) %collective-permute-start.25) | collective-permute-done | bytes 524320 | tf_op jit(solution)/shard_map/ppermute | solution.py:43
  195.8 1.1 shard_map.184
  197.0 7.9 %all-to-all-start.3 = ((bf16[64,8,1024]{2,1,0:T(8,128)(2,1)}), bf16[64,8,1024]{2,1,0:T(8,128)(2,1)S(1)}, u32[]{:S(2)}, u32[]{:S(2)}) async-start(bf16[64,8,1024]{2,1,0:T(8,128)(2,1)} %bitcast.27), calls=%async_computation.3 | async-start | bytes 2097152 | tf_op jit(solution)/shard_map/all_to_all | solution.py:452
  205.5 0.4 and_select_fusion
  206.0 0.5 select_n.156
  206.6 27.2 %all-to-all-done.3 = bf16[64,8,1024]{2,1,0:T(8,128)(2,1)S(1)} async-done(((bf16[64,8,1024]{2,1,0:T(8,128)(2,1)}), bf16[64,8,1024]{2,1,0:T(8,128)(2,1)S(1)}, u32[]{:S(2)}, u32[]{:S(2)}) %all-to-all-start.3) | async-done | bytes 1048608 | tf_op jit(solution)/shard_map/all_to_all | solution.py:452
  233.8 0.9 shard_map.185
  (75 shorter events, 3.0 us)
Async XLA Ops:
  1.9 18.0 %collective-permute-start.4 = (bf16[128,2048]{1,0:T(8,128)(2,1)S(1)}, bf16[128,2048]{1,0:T(8,128)(2,1)S(1)}, u32[]{:S(2)}, u32[]{:S(2)}) collective-permute-start(bf16[128,2048]{1,0:T(8,128)(2,1)S(1)} %get-tuple-element.89), channel_id=1, source_target_pairs={{0,1},{1,0},{2,3},{3,2},{4,5},{5,4},{6,7},{7,6},{8,9},{9,8},{10,11... | collective-permute-start | bytes 1572872 | tf_op jit(solution)/shard_map/ppermute | solution.py:51
  4.1 6.5 %collective-permute-start = (s32[8]{0:T(128)S(1)}, s32[8]{0:T(128)S(1)}, u32[]{:S(2)}, u32[]{:S(2)}) collective-permute-start(s32[8]{0:T(128)S(1)} %get-tuple-element.95), channel_id=1, source_target_pairs={{0,64},{64,128},{128,192},{192,0},{1,65},{65,129},{129,193},{193,1... | collective-permute-start | bytes 104 | tf_op jit(solution)/shard_map/ppermute | solution.py:43
  6.0 5.0 %collective-permute-start.1 = (s32[8]{0:T(128)S(1)}, s32[8]{0:T(128)S(1)}, u32[]{:S(2)}, u32[]{:S(2)}) collective-permute-start(s32[8]{0:T(128)S(1)} %get-tuple-element.94), channel_id=1, source_target_pairs={{0,128},{64,192},{128,0},{192,64},{1,129},{65,193},{129,1},{193,65... | collective-permute-start | bytes 104 | tf_op jit(solution)/shard_map/ppermute | solution.py:43
  6.9 4.8 %collective-permute-start.2 = (s32[8]{0:T(128)S(1)}, s32[8]{0:T(128)S(1)}, u32[]{:S(2)}, u32[]{:S(2)}) collective-permute-start(s32[8]{0:T(128)S(1)} %get-tuple-element.93), channel_id=1, source_target_pairs={{0,192},{64,0},{128,64},{192,128},{1,193},{65,1},{129,65},{193,129... | collective-permute-start | bytes 104 | tf_op jit(solution)/shard_map/ppermute | solution.py:43
  10.6 1.1 copy-start.11
  11.1 0.6 copy-start.12
  11.6 0.5 copy-start.13
  14.8 7.1 %collective-permute-start.3 = (bf16[4,2,16,512]{3,2,1,0:T(8,128)(2,1)}, bf16[4,2,16,512]{3,2,1,0:T(8,128)(2,1)S(1)}, u32[]{:S(2)}, u32[]{:S(2)}) collective-permute-start(bf16[4,2,16,512]{3,2,1,0:T(8,128)(2,1)} %get-tuple-element.44), channel_id=1, source_target_pairs={{0,192},{64,0},{128,64},{192,128},{1,193},{65,1},{129,65},{193,129... | collective-permute-start | bytes 393224 | tf_op jit(solution)/shard_map/ppermute | solution.py:43
  16.6 11.7 %collective-permute-start.5 = (bf16[4,2,16,512]{3,2,1,0:T(8,128)(2,1)}, bf16[4,2,16,512]{3,2,1,0:T(8,128)(2,1)S(1)}, u32[]{:S(2)}, u32[]{:S(2)}) collective-permute-start(bf16[4,2,16,512]{3,2,1,0:T(8,128)(2,1)} %get-tuple-element.51), channel_id=1, source_target_pairs={{0,128},{64,192},{128,0},{192,64},{1,129},{65,193},{129,1},{193,65... | collective-permute-start | bytes 393224 | tf_op jit(solution)/shard_map/ppermute | solution.py:43
  18.7 9.6 %collective-permute-start.6 = (bf16[4,2,16,512]{3,2,1,0:T(8,128)(2,1)}, bf16[4,2,16,512]{3,2,1,0:T(8,128)(2,1)S(1)}, u32[]{:S(2)}, u32[]{:S(2)}) collective-permute-start(bf16[4,2,16,512]{3,2,1,0:T(8,128)(2,1)} %get-tuple-element.52), channel_id=1, source_target_pairs={{0,64},{64,128},{128,192},{192,0},{1,65},{65,129},{129,193},{193,1... | collective-permute-start | bytes 393224 | tf_op jit(solution)/shard_map/ppermute | solution.py:43
  21.9 6.4 %copy-start.5 = (bf16[4,2,16,512]{3,2,1,0:T(8,128)(2,1)}, bf16[4,2,16,512]{3,2,1,0:T(8,128)(2,1)S(1)}, u32[]{:S(2)}) copy-start(bf16[4,2,16,512]{3,2,1,0:T(8,128)(2,1)S(1)} %collective-permute-done.3.b1) | copy-start | bytes 393220
  22.0 30.1 %collective-permute-start.7 = (bf16[256,512]{1,0:T(8,128)(2,1)S(1)}, bf16[256,512]{1,0:T(8,128)(2,1)S(1)}, u32[]{:S(2)}, u32[]{:S(2)}) collective-permute-start(bf16[256,512]{1,0:T(8,128)(2,1)S(1)} %get-tuple-element.86), channel_id=1, source_target_pairs={{0,2},{1,3},{2,4},{3,5},{4,6},{5,7},{6,0},{7,1},{8,10},{9,11},{10,... | collective-permute-start | bytes 786440 | tf_op jit(solution)/shard_map/ppermute | solution.py:51
  23.6 28.6 %collective-permute-start.8 = (bf16[256,512]{1,0:T(8,128)(2,1)S(1)}, bf16[256,512]{1,0:T(8,128)(2,1)S(1)}, u32[]{:S(2)}, u32[]{:S(2)}) collective-permute-start(bf16[256,512]{1,0:T(8,128)(2,1)S(1)} %get-tuple-element.85), channel_id=1, source_target_pairs={{0,4},{1,5},{2,6},{3,7},{4,0},{5,1},{6,2},{7,3},{8,12},{9,13},{10,... | collective-permute-start | bytes 786440 | tf_op jit(solution)/shard_map/ppermute | solution.py:51
  26.1 26.0 %collective-permute-start.9 = (bf16[256,512]{1,0:T(8,128)(2,1)S(1)}, bf16[256,512]{1,0:T(8,128)(2,1)S(1)}, u32[]{:S(2)}, u32[]{:S(2)}) collective-permute-start(bf16[256,512]{1,0:T(8,128)(2,1)S(1)} %get-tuple-element.84), channel_id=1, source_target_pairs={{0,6},{1,7},{2,0},{3,1},{4,2},{5,3},{6,4},{7,5},{8,14},{9,15},{10,... | collective-permute-start | bytes 786440 | tf_op jit(solution)/shard_map/ppermute | solution.py:51
  28.3 0.7 copy-start.6
  28.3 0.7 copy-start.7
  29.0 41.5 %copy-start.8 = (s32[8,8]{1,0:T(8,128)S(1)}, s32[8,8]{1,0:T(8,128)}, u32[]{:S(2)}) copy-start(s32[8,8]{1,0:T(8,128)} %param.28) | copy-start | bytes 772
  34.4 39.2 %copy-start.10 = (bf16[4096]{0:T(1024)(128)(2,1)S(1)}, bf16[4096]{0:T(1024)(128)(2,1)}, u32[]{:S(2)}) copy-start(bf16[4096]{0:T(1024)(128)(2,1)} %param.27) | copy-start | bytes 24580
  34.4 53.6 %copy-start.3 = (bf16[8,4096]{1,0:T(8,128)(2,1)S(1)}, bf16[8,4096]{1,0:T(8,128)(2,1)}, u32[]{:S(2)}) copy-start(bf16[8,4096]{1,0:T(8,128)(2,1)} %residual_ref.1) | copy-start | bytes 196612
  52.2 7.7 %collective-permute-start.10 = (bf16[64,1024]{1,0:T(8,128)(2,1)S(1)}, bf16[64,1024]{1,0:T(8,128)(2,1)S(1)}, u32[]{:S(2)}, u32[]{:S(2)}) collective-permute-start(bf16[64,1024]{1,0:T(8,128)(2,1)S(1)} %bitcast.50), channel_id=1, source_target_pairs={{0,2},{1,3},{2,4},{3,5},{4,6},{5,7},{6,0},{7,1},{8,10},{9,11},{10,... | collective-permute-start | bytes 393224 | tf_op jit(solution)/shard_map/ppermute | solution.py:51
  52.5 7.3 %collective-permute-start.11 = (bf16[64,1024]{1,0:T(8,128)(2,1)S(1)}, bf16[64,1024]{1,0:T(8,128)(2,1)S(1)}, u32[]{:S(2)}, u32[]{:S(2)}) collective-permute-start(bf16[64,1024]{1,0:T(8,128)(2,1)S(1)} %bitcast.51), channel_id=1, source_target_pairs={{0,4},{1,5},{2,6},{3,7},{4,0},{5,1},{6,2},{7,3},{8,12},{9,13},{10,... | collective-permute-start | bytes 393224 | tf_op jit(solution)/shard_map/ppermute | solution.py:51
  53.7 7.0 %collective-permute-start.12 = (bf16[64,1024]{1,0:T(8,128)(2,1)S(1)}, bf16[64,1024]{1,0:T(8,128)(2,1)S(1)}, u32[]{:S(2)}, u32[]{:S(2)}) collective-permute-start(bf16[64,1024]{1,0:T(8,128)(2,1)S(1)} %bitcast.52), channel_id=1, source_target_pairs={{0,6},{1,7},{2,0},{3,1},{4,2},{5,3},{6,4},{7,5},{8,14},{9,15},{10,... | collective-permute-start | bytes 393224 | tf_op jit(solution)/shard_map/ppermute | solution.py:51
  60.8 2.0 collective-permute-start.13
  64.8 23.2 %all-to-all-start.1 = ((bf16[64,8,512]{2,1,0:T(8,128)(2,1)}), bf16[64,8,512]{2,1,0:T(8,128)(2,1)}, u32[]{:S(2)}, u32[]{:S(2)}) async-start(bf16[64,8,512]{2,1,0:T(8,128)(2,1)} %bitcast.16), calls=%async_computation.1 | async-start | bytes 1048576 | tf_op jit(solution)/shard_map/all_to_all | solution.py:264
  70.8 58.8 %copy-start = (bf16[1,4096,384]{2,1,0:T(8,128)(2,1)S(1)}, bf16[1,4096,384]{2,1,0:T(8,128)(2,1)}, u32[]{:S(2)}) copy-start(bf16[1,4096,384]{2,1,0:T(8,128)(2,1)} %param.30) | copy-start | bytes 9437188
  70.8 58.9 %copy-start.2 = (bf16[256,256]{1,0:T(8,128)(2,1)S(1)}, bf16[256,256]{1,0:T(8,128)(2,1)}, u32[]{:S(2)}) copy-start(bf16[256,256]{1,0:T(8,128)(2,1)} %constant.113.clone.order_ref) | copy-start | bytes 393220
  124.3 16.2 %collective-permute-start.14 = (bf16[256,1024]{1,0:T(8,128)(2,1)S(1)}, bf16[256,1024]{1,0:T(8,128)(2,1)S(1)}, u32[]{:S(2)}, u32[]{:S(2)}) collective-permute-start(bf16[256,1024]{1,0:T(8,128)(2,1)S(1)} %get-tuple-element.83), channel_id=1, source_target_pairs={{0,192},{64,0},{128,64},{192,128},{1,193},{65,1},{129,65},{193,129... | collective-permute-start | bytes 1572872 | tf_op jit(solution)/shard_map/ppermute | solution.py:43
  124.4 16.1 %collective-permute-start.15 = (bf16[256,1024]{1,0:T(8,128)(2,1)S(1)}, bf16[256,1024]{1,0:T(8,128)(2,1)S(1)}, u32[]{:S(2)}, u32[]{:S(2)}) collective-permute-start(bf16[256,1024]{1,0:T(8,128)(2,1)S(1)} %get-tuple-element.82), channel_id=1, source_target_pairs={{0,64},{64,128},{128,192},{192,0},{1,65},{65,129},{129,193},{193,1... | collective-permute-start | bytes 1572872 | tf_op jit(solution)/shard_map/ppermute | solution.py:43
  127.6 23.6 %collective-permute-start.18 = (bf16[256,1024]{1,0:T(8,128)(2,1)S(1)}, bf16[256,1024]{1,0:T(8,128)(2,1)S(1)}, u32[]{:S(2)}, u32[]{:S(2)}) collective-permute-start(bf16[256,1024]{1,0:T(8,128)(2,1)S(1)} %get-tuple-element.83), channel_id=1, source_target_pairs={{0,64},{64,128},{128,192},{192,0},{1,65},{65,129},{129,193},{193,1... | collective-permute-start | bytes 1572872 | tf_op jit(solution)/shard_map/ppermute | solution.py:43
  127.7 24.0 %collective-permute-start.19 = (bf16[256,1024]{1,0:T(8,128)(2,1)S(1)}, bf16[256,1024]{1,0:T(8,128)(2,1)S(1)}, u32[]{:S(2)}, u32[]{:S(2)}) collective-permute-start(bf16[256,1024]{1,0:T(8,128)(2,1)S(1)} %get-tuple-element.82), channel_id=1, source_target_pairs={{0,192},{64,0},{128,64},{192,128},{1,193},{65,1},{129,65},{193,129... | collective-permute-start | bytes 1572872 | tf_op jit(solution)/shard_map/ppermute | solution.py:43
  135.8 27.8 %copy-start.1 = (bf16[1,4096,384]{2,1,0:T(8,128)(2,1)S(1)}, bf16[1,4096,384]{2,1,0:T(8,128)(2,1)}, u32[]{:S(2)}) copy-start(bf16[1,4096,384]{2,1,0:T(8,128)(2,1)} %param.30) | copy-start | bytes 9437188
  140.5 23.2 %collective-permute-start.16 = (bf16[256,1024]{1,0:T(8,128)(2,1)S(1)}, bf16[256,1024]{1,0:T(8,128)(2,1)S(1)}, u32[]{:S(2)}, u32[]{:S(2)}) collective-permute-start(bf16[256,1024]{1,0:T(8,128)(2,1)S(1)} %collective-permute-done.14.refs_2_), channel_id=1, source_target_pairs={{0,192},{64,0},{128,64},{192,128},{1,193},{65,1},{129,65},{193,129... | collective-permute-start | bytes 1572872 | tf_op jit(solution)/shard_map/ppermute | solution.py:43
  140.6 23.0 %collective-permute-start.17 = (bf16[256,1024]{1,0:T(8,128)(2,1)S(1)}, bf16[256,1024]{1,0:T(8,128)(2,1)S(1)}, u32[]{:S(2)}, u32[]{:S(2)}) collective-permute-start(bf16[256,1024]{1,0:T(8,128)(2,1)S(1)} %collective-permute-done.15.refs_1_), channel_id=1, source_target_pairs={{0,64},{64,128},{128,192},{192,0},{1,65},{65,129},{129,193},{193,1... | collective-permute-start | bytes 1572872 | tf_op jit(solution)/shard_map/ppermute | solution.py:43
  160.2 12.5 %collective-permute-start.22 = (bf16[256,1024]{1,0:T(8,128)(2,1)S(1)}, bf16[256,1024]{1,0:T(8,128)(2,1)S(1)}, u32[]{:S(2)}, u32[]{:S(2)}) collective-permute-start(bf16[256,1024]{1,0:T(8,128)(2,1)S(1)} %get-tuple-element.70), channel_id=1, source_target_pairs={{0,192},{64,0},{128,64},{192,128},{1,193},{65,1},{129,65},{193,129... | collective-permute-start | bytes 1572872 | tf_op jit(solution)/shard_map/ppermute | solution.py:43
  160.5 14.2 %collective-permute-start.23 = (bf16[256,1024]{1,0:T(8,128)(2,1)S(1)}, bf16[256,1024]{1,0:T(8,128)(2,1)S(1)}, u32[]{:S(2)}, u32[]{:S(2)}) collective-permute-start(bf16[256,1024]{1,0:T(8,128)(2,1)S(1)} %get-tuple-element.71), channel_id=1, source_target_pairs={{0,64},{64,128},{128,192},{192,0},{1,65},{65,129},{129,193},{193,1... | collective-permute-start | bytes 1572872 | tf_op jit(solution)/shard_map/ppermute | solution.py:43
  169.8 12.9 %collective-permute-start.20 = (bf16[256,1024]{1,0:T(8,128)(2,1)S(1)}, bf16[256,1024]{1,0:T(8,128)(2,1)S(1)}, u32[]{:S(2)}, u32[]{:S(2)}) collective-permute-start(bf16[256,1024]{1,0:T(8,128)(2,1)S(1)} %get-tuple-element.67), channel_id=1, source_target_pairs={{0,64},{64,128},{128,192},{192,0},{1,65},{65,129},{129,193},{193,1... | collective-permute-start | bytes 1572872 | tf_op jit(solution)/shard_map/ppermute | solution.py:43
  171.9 11.7 %collective-permute-start.21 = (bf16[256,1024]{1,0:T(8,128)(2,1)S(1)}, bf16[256,1024]{1,0:T(8,128)(2,1)S(1)}, u32[]{:S(2)}, u32[]{:S(2)}) collective-permute-start(bf16[256,1024]{1,0:T(8,128)(2,1)S(1)} %get-tuple-element.68), channel_id=1, source_target_pairs={{0,192},{64,0},{128,64},{192,128},{1,193},{65,1},{129,65},{193,129... | collective-permute-start | bytes 1572872 | tf_op jit(solution)/shard_map/ppermute | solution.py:43
  183.7 12.1 %collective-permute-start.25 = (bf16[256,1024]{1,0:T(8,128)(2,1)S(1)}, bf16[256,1024]{1,0:T(8,128)(2,1)S(1)}, u32[]{:S(2)}, u32[]{:S(2)}) collective-permute-start(bf16[256,1024]{1,0:T(8,128)(2,1)S(1)} %add_convert_fusion), channel_id=1, source_target_pairs={{0,192},{64,0},{128,64},{192,128},{1,193},{65,1},{129,65},{193,129... | collective-permute-start | bytes 1572872 | tf_op jit(solution)/shard_map/ppermute | solution.py:43
  184.3 20.8 %copy-start.9 = (f32[8,8]{1,0:T(8,128)S(1)}, f32[8,8]{1,0:T(8,128)}, u32[]{:S(2)}) copy-start(f32[8,8]{1,0:T(8,128)} %param.29) | copy-start | bytes 772
  184.3 11.5 %collective-permute-start.24 = (bf16[256,1024]{1,0:T(8,128)(2,1)S(1)}, bf16[256,1024]{1,0:T(8,128)(2,1)S(1)}, u32[]{:S(2)}, u32[]{:S(2)}) collective-permute-start(bf16[256,1024]{1,0:T(8,128)(2,1)S(1)} %add_convert_fusion.1), channel_id=1, source_target_pairs={{0,64},{64,128},{128,192},{192,0},{1,65},{65,129},{129,193},{193,1... | collective-permute-start | bytes 1572872 | tf_op jit(solution)/shard_map/ppermute | solution.py:43
  197.0 36.8 %copy-start.4 = (bf16[8,4096]{1,0:T(8,128)(2,1)S(1)}, bf16[8,4096]{1,0:T(8,128)(2,1)}, u32[]{:S(2)}) copy-start(bf16[8,4096]{1,0:T(8,128)(2,1)} %get-tuple-element.38.attended_ref) | copy-start | bytes 196612
  197.0 36.8 %all-to-all-start.3 = ((bf16[64,8,1024]{2,1,0:T(8,128)(2,1)}), bf16[64,8,1024]{2,1,0:T(8,128)(2,1)S(1)}, u32[]{:S(2)}, u32[]{:S(2)}) async-start(bf16[64,8,1024]{2,1,0:T(8,128)(2,1)} %bitcast.27), calls=%async_computation.3 | async-start | bytes 2097152 | tf_op jit(solution)/shard_map/all_to_all | solution.py:452

commit v2 on v1

--- a/solution.py
+++ b/solution.py
@@ -337,7 +337,7 @@
             ).astype(jnp.bfloat16)
 
 
-def expert(arrays, w_gate, w_up, w_down, order):
+def expert(arrays, w_gate, w_up, w_down, order, share=1):
     layout = [a.shape[0] // HALF for a in arrays]
     rows = sum(layout) * HALF // PARTS
     span = PER_STEP * PART
@@ -358,7 +358,9 @@
         ],
         compiler_params=pltpu.CompilerParams(vmem_limit_bytes=BIG),
         cost_estimate=pl.CostEstimate(
-            flops=6 * rows * D * FF_PART, bytes_accessed=6 * D * FF_PART + 4 * rows * D, transcendentals=0
+            flops=6 * rows * D * FF_PART // share,
+            bytes_accessed=(6 * D * FF_PART + 4 * rows * D) // share,
+            transcendentals=0,
         ),
     )(order, *arrays, w_gate, w_up, w_down)
 
@@ -460,24 +462,28 @@
     (own,) = expert([mine], *weights)
     right_a, left_b, own = tie((right_a, left_b, own))
     far_a, far_b = shift_pool(right_a, -1), shift_pool(left_b, 1)
-    to_left_a, to_left_b, to_right_a, to_right_b = expert([left_a, left_b, right_a, right_b], *weights)
-    from_left_b, from_right_a = shift_pool(to_right_b, 1), shift_pool(to_left_a, -1)
-    far_a, far_b, to_left_b, to_right_a = tie((far_a, far_b, to_left_b, to_right_a))
+    to_right_a, to_left_b = expert([right_a, left_b], *weights, share=64)
+    from_left_a, from_right_b = shift_pool(to_right_a, 1), shift_pool(to_left_b, -1)
+    far_a, far_b, left_a, right_b, to_right_a, to_left_b = tie(
+        (far_a, far_b, left_a, right_b, to_right_a, to_left_b)
+    )
     to_far_a, to_far_b = expert([far_a, far_b], *weights)
-    over_a, over_b = shift_pool(to_far_a, 1), shift_pool(to_far_b, -1)
+    over_a, over_b = shift_pool(to_far_a, -1), shift_pool(to_far_b, 1)
+    left_a, right_b, to_far_a, to_far_b = tie((left_a, right_b, to_far_a, to_far_b))
+    to_left_a, to_right_b = expert([left_a, right_b], *weights)
 
     def wide(value):
         return value.astype(jnp.float32)
 
-    base_a, base_b = wide(own[:HALF]) + wide(from_right_a), wide(own[HALF:]) + wide(from_left_b)
+    base_a, base_b = wide(own[:HALF]) + wide(from_left_a), wide(own[HALF:]) + wide(from_right_b)
     over_a, over_b, base_a, base_b = tie((over_a, over_b, base_a, base_b))
-    from_left_a = shift_pool((wide(to_right_a) + wide(over_a)).astype(jnp.bfloat16), 1)
-    from_right_b = shift_pool((wide(to_left_b) + wide(over_b)).astype(jnp.bfloat16), -1)
+    from_right_a = shift_pool((wide(to_left_a) + wide(over_a)).astype(jnp.bfloat16), -1)
+    from_left_b = shift_pool((wide(to_right_b) + wide(over_b)).astype(jnp.bfloat16), 1)
     summed = pl.pallas_call(
         sum_kernel,
         out_shape=jax.ShapeDtypeStruct(message, jnp.bfloat16),
         compiler_params=pltpu.CompilerParams(vmem_limit_bytes=BIG),
-    )(base_a, base_b, from_left_a, from_right_b)
+    )(base_a, base_b, from_right_a, from_left_b)
     returned = exchange(summed)
     layer_out = pl.pallas_call(
         finish_kernel,

time: 239 us -> 239 us (level); the launches traced: 235 us -> 238 us
  Pallas kernels: 34.9 us -> 38.7 us
    pallas_call x3 -> x4, Pallas kernels: 20.9 us -> 24.6 us  [expert(): pl.pallas_call(functools.partial(expert_kernel, layout), grid=(2 * STEPS,...]
  transfers between devices with their start and end apart: 28 -> 28, of which waited for: 16 -> 13; matrix products, arithmetic and copies ran while one was open for 5% -> 5% of each run, Pallas kernels for 12% -> 14%
where the time goes in v2:
time: 239 us; the launch traced here: 238 us
  waiting for transfers between devices  82.8 us (35%)
  blocking collectives  52.4 us (22%)
  starting transfers between devices  48.7 us (20%)
  Pallas kernels  38.7 us (16%)
  local copies, waits for them, and re-layouts  7.92 us (3%)
  other arithmetic  6.23 us (3%)
    all_to_all x1, blocking collectives, exchange(): lax.all_to_all(parted, 'ep', split_axis=0, concat_axis=0, tiled=True)  34.5 us
    ppermute x18, waiting for transfers between devices, shift_pool(): lax.ppermute(value, 'pool', [(i, (i + step) % N_POOL) for i in range(N_PO...  34.2 us
    all_to_all x1, waiting for transfers between devices, exchange(): lax.all_to_all(parted, 'ep', split_axis=0, concat_axis=0, tiled=True)  27.2 us
    ppermute x18, starting transfers between devices, shift_pool(): lax.ppermute(value, 'pool', [(i, (i + step) % N_POOL) for i in range(N_PO...  26.4 us
    pallas_call x4, Pallas kernels, expert(): pl.pallas_call(functools.partial(expert_kernel, layout), grid=(2 * STEPS,...  24.6 us
    all_to_all x1, blocking collectives, project(): lax.all_to_all(context.reshape(N_Z, ROWS, DEEP), 'ep', split_axis=0, conc...  17.9 us
    all_to_all x1, waiting for transfers between devices, project(): lax.all_to_all(product.reshape(N_EP, ROWS, CHUNK), 'ep', split_axis=0, co...  14.3 us
    ppermute x8, starting transfers between devices, shift_ep(): return lax.ppermute(value, 'ep', pairs)  9.39 us
  transfers between devices with their start and end apart: 28, of which 13 were waited for; matrix products, arithmetic and copies ran while one was open for 5% of the time, Pallas kernels for 14%

profile of v2, /device:TPU:24, one launch (start us, length us, event | category | flops | bytes accessed | tf_op | source)
XLA Modules:
  0.0 237.7 jit_solution(9793706885692973009)
XLA Ops:
  0.7 1.3 dynamic-slice_bitcast_fusion
  2.0 0.7 add_select_fusion
  2.7 0.7 broadcast_compare_fusion.1
  3.6 0.5 slice_bitcast_fusion.2
  4.1 2.0 collective-permute-start
  6.0 0.9 collective-permute-start.1
  6.9 0.8 select_reduce_fusion.2
  7.7 0.7 pad_add_fusion
  8.4 0.6 reshape.156.facts_ref
  9.0 1.6 copy.46
  10.6 0.5 collective-permute-done.1.refs_2_
  11.1 0.6 collective-permute-done.2.refs_3_
  11.6 0.5 copy-done.12
  12.2 2.7 %shard_map.176 = (bf16[4,2,16,512]{3,2,1,0:T(8,128)(2,1)}, bf16[4,2,16,512]{3,2,1,0:T(8,128)(2,1)}, bf16[4,2,16,512]{3,2,1,0:T(8,128)(2,1)}, bf16[4,2,16,512]{3,2,1,0:T(8,128)(2,1)}) custom-call(s32[8]{0:T(128)} %get-tuple-element.42.refs_0_, s32[8]{0:T(128)} %copy-done.10, s32[8]{0:T(128)} %copy-done.11, s32[8]{0:T(128)} %copy-done.12, ...), custom_call_target="tpu_custom_call" | custom-call | bytes 1048576 | tf_op jit(solution)/shard_map/pallas_call | solution.py:105
  14.8 1.7 collective-permute-start.3
  16.6 2.0 collective-permute-start.5
  18.6 1.3 collective-permute-start.6
  20.1 1.7 collective-permute-done.3.b1
  21.9 1.8 collective-permute-start.7
  23.7 3.2 %collective-permute-start.8 = (bf16[256,512]{1,0:T(8,128)(2,1)S(1)}, bf16[256,512]{1,0:T(8,128)(2,1)S(1)}, u32[]{:S(2)}, u32[]{:S(2)}) collective-permute-start(bf16[256,512]{1,0:T(8,128)(2,1)S(1)} %get-tuple-element.89), channel_id=1, source_target_pairs={{0,4},{1,5},{2,6},{3,7},{4,0},{5,1},{6,2},{7,3},{8,12},{9,13},{10,... | collective-permute-start | bytes 786440 | tf_op jit(solution)/shard_map/ppermute | solution.py:51
  26.9 0.9 collective-permute-start.9
  27.8 0.6 copy-done.5
  28.5 5.4 %shard_map.177 = bf16[64,1024]{1,0:T(8,128)(2,1)} custom-call(s32[56]{0:T(128)} %reshape.156.facts_ref, bf16[8,64,128]{2,1,0:T(8,128)(2,1)} %bitcast.66, bf16[8,512]{1,0:T(8,128)(2,1)} %key_ref.1, bf16[8,512]{1,0:T(8,128)(2,1)} %value_ref.1, bf16[8,2,64,512]{3,2,1,0:T(8,128)(2,1)} %resident_ref.1, bf16[4,2,16,512]{3,2,1,0:T(8,128)(2,1)} %get-tuple-element.51.b0, ...), custom_call_target="tpu_custom_call" | custom-call | flops 268435456 | bytes 3145728 | tf_op jit(solution)/shard_map/pallas_call | solution.py:177
  33.9 17.9 %all_to_all.20 = bf16[8,8,1024]{2,1,0:T(8,128)(2,1)S(1)} all-to-all(bf16[8,8,1024]{2,1,0:T(8,128)(2,1)} %bitcast.67), channel_id=1, replica_groups={{0,8,16,24,32,40,48,56},{1,9,17,25,33,41,49,57},{2,10,18,26,34,42,50,58..., dimensions={0} | all-to-all | bytes 262144 | tf_op jit(solution)/shard_map/all_to_all | solution.py:240
  51.8 0.6 collective-permute-start.10
  52.4 1.0 collective-permute-start.11
  53.4 1.8 collective-permute-start.12
  55.2 4.3 %collective-permute-done.10.refs_1_ = bf16[64,1024]{1,0:T(8,128)(2,1)S(1)} collective-permute-done((bf16[64,1024]{1,0:T(8,128)(2,1)S(1)}, bf16[64,1024]{1,0:T(8,128)(2,1)S(1)}, u32[]{:S(2)}, u32[]{:S(2)}) %collective-permute-start.10) | collective-permute-done | bytes 131104 | tf_op jit(solution)/shard_map/ppermute | solution.py:51
  59.5 0.9 collective-permute-done.12.refs_3_
  60.6 1.8 collective-permute-done.13.other_ref
  62.4 2.1 shard_map.179
  64.5 5.7 %all-to-all-start.1 = ((bf16[64,8,512]{2,1,0:T(8,128)(2,1)}), bf16[64,8,512]{2,1,0:T(8,128)(2,1)}, u32[]{:S(2)}, u32[]{:S(2)}) async-start(bf16[64,8,512]{2,1,0:T(8,128)(2,1)} %bitcast.16), calls=%async_computation.1 | async-start | bytes 1048576 | tf_op jit(solution)/shard_map/all_to_all | solution.py:264
  70.8 1.2 select_convert_fusion
  71.9 1.4 convert_element_type.37.pick_ref
  73.4 14.3 %all-to-all-done.1 = bf16[64,8,512]{2,1,0:T(8,128)(2,1)} async-done(((bf16[64,8,512]{2,1,0:T(8,128)(2,1)}), bf16[64,8,512]{2,1,0:T(8,128)(2,1)}, u32[]{:S(2)}, u32[]{:S(2)}) %all-to-all-start.1) | async-done | bytes 524320 | tf_op jit(solution)/shard_map/all_to_all | solution.py:264
  87.7 1.8 shard_map.180
  89.4 34.5 %all_to_all.21 = bf16[64,8,1024]{2,1,0:T(8,128)(2,1)S(1)} all-to-all(bf16[64,8,1024]{2,1,0:T(8,128)(2,1)S(1)} %bitcast.50), channel_id=1, replica_groups=mesh['pool'=4,'ep'=64] {'ep'}, dimensions={0} | all-to-all | bytes 2097152 | tf_op jit(solution)/shard_map/all_to_all | solution.py:454
  124.1 3.2 %collective-permute-start.15 = (bf16[256,1024]{1,0:T(8,128)(2,1)S(1)}, bf16[256,1024]{1,0:T(8,128)(2,1)S(1)}, u32[]{:S(2)}, u32[]{:S(2)}) collective-permute-start(bf16[256,1024]{1,0:T(8,128)(2,1)S(1)} %get-tuple-element.86), channel_id=1, source_target_pairs={{0,64},{64,128},{128,192},{192,0},{1,65},{65,129},{129,193},{193,1... | collective-permute-start | bytes 1572872 | tf_op jit(solution)/shard_map/ppermute | solution.py:43
  127.3 0.5 collective-permute-start.18
  127.8 1.5 collective-permute-start.19
  129.3 6.1 %shard_map.181 = bf16[512,1024]{1,0:T(8,128)(2,1)S(1)} custom-call(bf16[256,256]{1,0:T(8,128)(2,1)S(1)} %copy-done.1, bf16[512,1024]{1,0:T(8,128)(2,1)S(1)} %bitcast.48, bf16[4096,384]{1,0:T(8,128)(2,1)S(1)} %bitcast.44, bf16[4096,384]{1,0:T(8,128)(2,1)} %bitcast.55, bf16[384,4096]{1,0:T(8,128)(2,1)} %bitcast.59), custom_call_target="tpu_custom_call" | custom-call | flops 1207959552 | bytes 11534336 | tf_op jit(solution)/shard_map/pallas_call | solution.py:346
  135.5 4.6 %collective-permute-done.14.refs_0_ = bf16[256,1024]{1,0:T(8,128)(2,1)S(1)} collective-permute-done((bf16[256,1024]{1,0:T(8,128)(2,1)S(1)}, bf16[256,1024]{1,0:T(8,128)(2,1)S(1)}, u32[]{:S(2)}, u32[]{:S(2)}) %collective-permute-start.14) | collective-permute-done | bytes 524320 | tf_op jit(solution)/shard_map/ppermute | solution.py:43
  140.1 1.5 collective-permute-start.16
  141.7 1.7 collective-permute-start.17
  143.4 6.2 %shard_map.182 = (bf16[256,1024]{1,0:T(8,128)(2,1)S(1)}, bf16[256,1024]{1,0:T(8,128)(2,1)S(1)}) custom-call(bf16[256,256]{1,0:T(8,128)(2,1)S(1)} %copy-done.1, bf16[256,1024]{1,0:T(8,128)(2,1)S(1)} %collective-permute-done.14.refs_0_, bf16[256,1024]{1,0:T(8,128)(2,1)S(1)} %collective-permute-done.15.refs_1_, bf16[4096,384]{1,0:T(8,128)(2,1)S(1)} %bitcast.45, ...), custom_call_target="tpu_custom_call" | custom-call | flops 18874368 | bytes 180224 | tf_op jit(solution)/shard_map/pallas_call | solution.py:346
  149.5 2.1 collective-permute-start.22
  151.6 1.3 collective-permute-start.23
  152.9 9.7 %collective-permute-done.16.refs_0_ = bf16[256,1024]{1,0:T(8,128)(2,1)S(1)} collective-permute-done((bf16[256,1024]{1,0:T(8,128)(2,1)S(1)}, bf16[256,1024]{1,0:T(8,128)(2,1)S(1)}, u32[]{:S(2)}, u32[]{:S(2)}) %collective-permute-start.16) | collective-permute-done | bytes 524320 | tf_op jit(solution)/shard_map/ppermute | solution.py:43
  162.6 6.2 %shard_map.183 = (bf16[256,1024]{1,0:T(8,128)(2,1)S(1)}, bf16[256,1024]{1,0:T(8,128)(2,1)S(1)}) custom-call(bf16[256,256]{1,0:T(8,128)(2,1)S(1)} %copy-done.1, bf16[256,1024]{1,0:T(8,128)(2,1)S(1)} %collective-permute-done.16.refs_0_, bf16[256,1024]{1,0:T(8,128)(2,1)S(1)} %collective-permute-done.17.refs_1_, bf16[4096,384]{1,0:T(8,128)(2,1)S(1)} %bitcast.46, ...), custom_call_target="tpu_custom_call" | custom-call | flops 1207959552 | bytes 11534336 | tf_op jit(solution)/shard_map/pallas_call | solution.py:346
  168.8 1.6 collective-permute-start.20
  170.4 1.8 collective-permute-start.21
  172.2 6.2 %shard_map.184 = (bf16[256,1024]{1,0:T(8,128)(2,1)S(1)}, bf16[256,1024]{1,0:T(8,128)(2,1)S(1)}) custom-call(bf16[256,256]{1,0:T(8,128)(2,1)S(1)} %copy-done.1, bf16[256,1024]{1,0:T(8,128)(2,1)S(1)} %collective-permute-done.18.refs_0_, bf16[256,1024]{1,0:T(8,128)(2,1)S(1)} %collective-permute-done.19.refs_1_, bf16[4096,384]{1,0:T(8,128)(2,1)S(1)} %bitcast.47, ...), custom_call_target="tpu_custom_call" | custom-call | flops 1207959552 | bytes 11534336 | tf_op jit(solution)/shard_map/pallas_call | solution.py:346
  178.4 0.4 convert_add_fusion
  178.8 4.4 %collective-permute-done.20 = bf16[256,1024]{1,0:T(8,128)(2,1)S(1)} collective-permute-done((bf16[256,1024]{1,0:T(8,128)(2,1)S(1)}, bf16[256,1024]{1,0:T(8,128)(2,1)S(1)}, u32[]{:S(2)}, u32[]{:S(2)}) %collective-permute-start.20) | collective-permute-done | bytes 524320 | tf_op jit(solution)/shard_map/ppermute | solution.py:43
  183.2 0.2 add_convert_fusion
  183.4 3.0 %collective-permute-start.25 = (bf16[256,1024]{1,0:T(8,128)(2,1)S(1)}, bf16[256,1024]{1,0:T(8,128)(2,1)S(1)}, u32[]{:S(2)}, u32[]{:S(2)}) collective-permute-start(bf16[256,1024]{1,0:T(8,128)(2,1)S(1)} %add_convert_fusion), channel_id=1, source_target_pairs={{0,64},{64,128},{128,192},{192,0},{1,65},{65,129},{129,193},{193,1... | collective-permute-start | bytes 1572872 | tf_op jit(solution)/shard_map/ppermute | solution.py:43
  186.7 9.0 %collective-permute-done.25.more_b_ref = bf16[256,1024]{1,0:T(8,128)(2,1)S(1)} collective-permute-done((bf16[256,1024]{1,0:T(8,128)(2,1)S(1)}, bf16[256,1024]{1,0:T(8,128)(2,1)S(1)}, u32[]{:S(2)}, u32[]{:S(2)}) %collective-permute-start.25) | collective-permute-done | bytes 524320 | tf_op jit(solution)/shard_map/ppermute | solution.py:43
  195.7 3.7 %collective-permute-done.24.more_a_ref = bf16[256,1024]{1,0:T(8,128)(2,1)S(1)} collective-permute-done((bf16[256,1024]{1,0:T(8,128)(2,1)S(1)}, bf16[256,1024]{1,0:T(8,128)(2,1)S(1)}, u32[]{:S(2)}, u32[]{:S(2)}) %collective-permute-start.24) | collective-permute-done | bytes 524320 | tf_op jit(solution)/shard_map/ppermute | solution.py:43
  199.4 1.1 shard_map.185
  200.6 7.3 %all-to-all-start.3 = ((bf16[64,8,1024]{2,1,0:T(8,128)(2,1)}), bf16[64,8,1024]{2,1,0:T(8,128)(2,1)S(1)}, u32[]{:S(2)}, u32[]{:S(2)}) async-start(bf16[64,8,1024]{2,1,0:T(8,128)(2,1)} %bitcast.27), calls=%async_computation.3 | async-start | bytes 2097152 | tf_op jit(solution)/shard_map/all_to_all | solution.py:454
  208.5 0.4 and_select_fusion
  208.9 0.5 select_n.156
  209.5 27.2 %all-to-all-done.3 = bf16[64,8,1024]{2,1,0:T(8,128)(2,1)S(1)} async-done(((bf16[64,8,1024]{2,1,0:T(8,128)(2,1)}), bf16[64,8,1024]{2,1,0:T(8,128)(2,1)S(1)}, u32[]{:S(2)}, u32[]{:S(2)}) %all-to-all-start.3) | async-done | bytes 1048608 | tf_op jit(solution)/shard_map/all_to_all | solution.py:454
  236.7 0.9 shard_map.186
  (74 shorter events, 2.7 us)
Async XLA Ops:
  1.9 18.0 %collective-permute-start.4 = (bf16[128,2048]{1,0:T(8,128)(2,1)S(1)}, bf16[128,2048]{1,0:T(8,128)(2,1)S(1)}, u32[]{:S(2)}, u32[]{:S(2)}) collective-permute-start(bf16[128,2048]{1,0:T(8,128)(2,1)S(1)} %get-tuple-element.93), channel_id=1, source_target_pairs={{0,1},{1,0},{2,3},{3,2},{4,5},{5,4},{6,7},{7,6},{8,9},{9,8},{10,11... | collective-permute-start | bytes 1572872 | tf_op jit(solution)/shard_map/ppermute | solution.py:51
  4.1 6.5 %collective-permute-start = (s32[8]{0:T(128)S(1)}, s32[8]{0:T(128)S(1)}, u32[]{:S(2)}, u32[]{:S(2)}) collective-permute-start(s32[8]{0:T(128)S(1)} %get-tuple-element.99), channel_id=1, source_target_pairs={{0,64},{64,128},{128,192},{192,0},{1,65},{65,129},{129,193},{193,1... | collective-permute-start | bytes 104 | tf_op jit(solution)/shard_map/ppermute | solution.py:43
  6.0 5.0 %collective-permute-start.1 = (s32[8]{0:T(128)S(1)}, s32[8]{0:T(128)S(1)}, u32[]{:S(2)}, u32[]{:S(2)}) collective-permute-start(s32[8]{0:T(128)S(1)} %get-tuple-element.98), channel_id=1, source_target_pairs={{0,128},{64,192},{128,0},{192,64},{1,129},{65,193},{129,1},{193,65... | collective-permute-start | bytes 104 | tf_op jit(solution)/shard_map/ppermute | solution.py:43
  6.9 4.8 %collective-permute-start.2 = (s32[8]{0:T(128)S(1)}, s32[8]{0:T(128)S(1)}, u32[]{:S(2)}, u32[]{:S(2)}) collective-permute-start(s32[8]{0:T(128)S(1)} %get-tuple-element.97), channel_id=1, source_target_pairs={{0,192},{64,0},{128,64},{192,128},{1,193},{65,1},{129,65},{193,129... | collective-permute-start | bytes 104 | tf_op jit(solution)/shard_map/ppermute | solution.py:43
  10.6 1.1 copy-start.10
  11.1 0.6 copy-start.11
  11.6 0.5 copy-start.12
  14.8 7.0 %collective-permute-start.3 = (bf16[4,2,16,512]{3,2,1,0:T(8,128)(2,1)}, bf16[4,2,16,512]{3,2,1,0:T(8,128)(2,1)S(1)}, u32[]{:S(2)}, u32[]{:S(2)}) collective-permute-start(bf16[4,2,16,512]{3,2,1,0:T(8,128)(2,1)} %get-tuple-element.46), channel_id=1, source_target_pairs={{0,192},{64,0},{128,64},{192,128},{1,193},{65,1},{129,65},{193,129... | collective-permute-start | bytes 393224 | tf_op jit(solution)/shard_map/ppermute | solution.py:43
  16.6 11.2 %collective-permute-start.5 = (bf16[4,2,16,512]{3,2,1,0:T(8,128)(2,1)}, bf16[4,2,16,512]{3,2,1,0:T(8,128)(2,1)S(1)}, u32[]{:S(2)}, u32[]{:S(2)}) collective-permute-start(bf16[4,2,16,512]{3,2,1,0:T(8,128)(2,1)} %get-tuple-element.53), channel_id=1, source_target_pairs={{0,128},{64,192},{128,0},{192,64},{1,129},{65,193},{129,1},{193,65... | collective-permute-start | bytes 393224 | tf_op jit(solution)/shard_map/ppermute | solution.py:43
  18.6 9.2 %collective-permute-start.6 = (bf16[4,2,16,512]{3,2,1,0:T(8,128)(2,1)}, bf16[4,2,16,512]{3,2,1,0:T(8,128)(2,1)S(1)}, u32[]{:S(2)}, u32[]{:S(2)}) collective-permute-start(bf16[4,2,16,512]{3,2,1,0:T(8,128)(2,1)} %get-tuple-element.54), channel_id=1, source_target_pairs={{0,64},{64,128},{128,192},{192,0},{1,65},{65,129},{129,193},{193,1... | collective-permute-start | bytes 393224 | tf_op jit(solution)/shard_map/ppermute | solution.py:43
  21.8 6.0 %copy-start.4 = (bf16[4,2,16,512]{3,2,1,0:T(8,128)(2,1)}, bf16[4,2,16,512]{3,2,1,0:T(8,128)(2,1)S(1)}, u32[]{:S(2)}) copy-start(bf16[4,2,16,512]{3,2,1,0:T(8,128)(2,1)S(1)} %collective-permute-done.3.b1) | copy-start | bytes 393220
  21.9 29.9 %collective-permute-start.7 = (bf16[256,512]{1,0:T(8,128)(2,1)S(1)}, bf16[256,512]{1,0:T(8,128)(2,1)S(1)}, u32[]{:S(2)}, u32[]{:S(2)}) collective-permute-start(bf16[256,512]{1,0:T(8,128)(2,1)S(1)} %get-tuple-element.90), channel_id=1, source_target_pairs={{0,2},{1,3},{2,4},{3,5},{4,6},{5,7},{6,0},{7,1},{8,10},{9,11},{10,... | collective-permute-start | bytes 786440 | tf_op jit(solution)/shard_map/ppermute | solution.py:51
  23.7 28.2 %collective-permute-start.8 = (bf16[256,512]{1,0:T(8,128)(2,1)S(1)}, bf16[256,512]{1,0:T(8,128)(2,1)S(1)}, u32[]{:S(2)}, u32[]{:S(2)}) collective-permute-start(bf16[256,512]{1,0:T(8,128)(2,1)S(1)} %get-tuple-element.89), channel_id=1, source_target_pairs={{0,4},{1,5},{2,6},{3,7},{4,0},{5,1},{6,2},{7,3},{8,12},{9,13},{10,... | collective-permute-start | bytes 786440 | tf_op jit(solution)/shard_map/ppermute | solution.py:51
  26.9 25.0 %collective-permute-start.9 = (bf16[256,512]{1,0:T(8,128)(2,1)S(1)}, bf16[256,512]{1,0:T(8,128)(2,1)S(1)}, u32[]{:S(2)}, u32[]{:S(2)}) collective-permute-start(bf16[256,512]{1,0:T(8,128)(2,1)S(1)} %get-tuple-element.88), channel_id=1, source_target_pairs={{0,6},{1,7},{2,0},{3,1},{4,2},{5,3},{6,4},{7,5},{8,14},{9,15},{10,... | collective-permute-start | bytes 786440 | tf_op jit(solution)/shard_map/ppermute | solution.py:51
  27.8 0.7 copy-start.5
  27.8 0.7 copy-start.6
  28.5 41.7 %copy-start.7 = (s32[8,8]{1,0:T(8,128)S(1)}, s32[8,8]{1,0:T(8,128)}, u32[]{:S(2)}) copy-start(s32[8,8]{1,0:T(8,128)} %param.28) | copy-start | bytes 772
  33.9 39.4 %copy-start.9 = (bf16[4096]{0:T(1024)(128)(2,1)S(1)}, bf16[4096]{0:T(1024)(128)(2,1)}, u32[]{:S(2)}) copy-start(bf16[4096]{0:T(1024)(128)(2,1)} %param.27) | copy-start | bytes 24580
  33.9 53.8 %copy-start.2 = (bf16[8,4096]{1,0:T(8,128)(2,1)S(1)}, bf16[8,4096]{1,0:T(8,128)(2,1)}, u32[]{:S(2)}) copy-start(bf16[8,4096]{1,0:T(8,128)(2,1)} %residual_ref.1) | copy-start | bytes 196612
  51.8 7.7 %collective-permute-start.10 = (bf16[64,1024]{1,0:T(8,128)(2,1)S(1)}, bf16[64,1024]{1,0:T(8,128)(2,1)S(1)}, u32[]{:S(2)}, u32[]{:S(2)}) collective-permute-start(bf16[64,1024]{1,0:T(8,128)(2,1)S(1)} %bitcast.51), channel_id=1, source_target_pairs={{0,2},{1,3},{2,4},{3,5},{4,6},{5,7},{6,0},{7,1},{8,10},{9,11},{10,... | collective-permute-start | bytes 393224 | tf_op jit(solution)/shard_map/ppermute | solution.py:51
  52.4 7.1 %collective-permute-start.11 = (bf16[64,1024]{1,0:T(8,128)(2,1)S(1)}, bf16[64,1024]{1,0:T(8,128)(2,1)S(1)}, u32[]{:S(2)}, u32[]{:S(2)}) collective-permute-start(bf16[64,1024]{1,0:T(8,128)(2,1)S(1)} %bitcast.52), channel_id=1, source_target_pairs={{0,4},{1,5},{2,6},{3,7},{4,0},{5,1},{6,2},{7,3},{8,12},{9,13},{10,... | collective-permute-start | bytes 393224 | tf_op jit(solution)/shard_map/ppermute | solution.py:51
  53.4 7.0 %collective-permute-start.12 = (bf16[64,1024]{1,0:T(8,128)(2,1)S(1)}, bf16[64,1024]{1,0:T(8,128)(2,1)S(1)}, u32[]{:S(2)}, u32[]{:S(2)}) collective-permute-start(bf16[64,1024]{1,0:T(8,128)(2,1)S(1)} %bitcast.53), channel_id=1, source_target_pairs={{0,6},{1,7},{2,0},{3,1},{4,2},{5,3},{6,4},{7,5},{8,14},{9,15},{10,... | collective-permute-start | bytes 393224 | tf_op jit(solution)/shard_map/ppermute | solution.py:51
  60.4 2.0 collective-permute-start.13
  64.5 23.2 %all-to-all-start.1 = ((bf16[64,8,512]{2,1,0:T(8,128)(2,1)}), bf16[64,8,512]{2,1,0:T(8,128)(2,1)}, u32[]{:S(2)}, u32[]{:S(2)}) async-start(bf16[64,8,512]{2,1,0:T(8,128)(2,1)} %bitcast.16), calls=%async_computation.1 | async-start | bytes 1048576 | tf_op jit(solution)/shard_map/all_to_all | solution.py:264
  70.5 58.8 %copy-start = (bf16[1,4096,384]{2,1,0:T(8,128)(2,1)S(1)}, bf16[1,4096,384]{2,1,0:T(8,128)(2,1)}, u32[]{:S(2)}) copy-start(bf16[1,4096,384]{2,1,0:T(8,128)(2,1)} %param.30) | copy-start | bytes 9437188
  70.5 58.9 %copy-start.1 = (bf16[256,256]{1,0:T(8,128)(2,1)S(1)}, bf16[256,256]{1,0:T(8,128)(2,1)}, u32[]{:S(2)}) copy-start(bf16[256,256]{1,0:T(8,128)(2,1)} %constant.113.clone.order_ref) | copy-start | bytes 393220
  124.0 16.2 %collective-permute-start.14 = (bf16[256,1024]{1,0:T(8,128)(2,1)S(1)}, bf16[256,1024]{1,0:T(8,128)(2,1)S(1)}, u32[]{:S(2)}, u32[]{:S(2)}) collective-permute-start(bf16[256,1024]{1,0:T(8,128)(2,1)S(1)} %get-tuple-element.87), channel_id=1, source_target_pairs={{0,192},{64,0},{128,64},{192,128},{1,193},{65,1},{129,65},{193,129... | collective-permute-start | bytes 1572872 | tf_op jit(solution)/shard_map/ppermute | solution.py:43
  124.1 16.1 %collective-permute-start.15 = (bf16[256,1024]{1,0:T(8,128)(2,1)S(1)}, bf16[256,1024]{1,0:T(8,128)(2,1)S(1)}, u32[]{:S(2)}, u32[]{:S(2)}) collective-permute-start(bf16[256,1024]{1,0:T(8,128)(2,1)S(1)} %get-tuple-element.86), channel_id=1, source_target_pairs={{0,64},{64,128},{128,192},{192,0},{1,65},{65,129},{129,193},{193,1... | collective-permute-start | bytes 1572872 | tf_op jit(solution)/shard_map/ppermute | solution.py:43
  127.3 24.3 %collective-permute-start.18 = (bf16[256,1024]{1,0:T(8,128)(2,1)S(1)}, bf16[256,1024]{1,0:T(8,128)(2,1)S(1)}, u32[]{:S(2)}, u32[]{:S(2)}) collective-permute-start(bf16[256,1024]{1,0:T(8,128)(2,1)S(1)} %get-tuple-element.87), channel_id=1, source_target_pairs={{0,64},{64,128},{128,192},{192,0},{1,65},{65,129},{129,193},{193,1... | collective-permute-start | bytes 1572872 | tf_op jit(solution)/shard_map/ppermute | solution.py:43
  127.8 25.1 %collective-permute-start.19 = (bf16[256,1024]{1,0:T(8,128)(2,1)S(1)}, bf16[256,1024]{1,0:T(8,128)(2,1)S(1)}, u32[]{:S(2)}, u32[]{:S(2)}) collective-permute-start(bf16[256,1024]{1,0:T(8,128)(2,1)S(1)} %get-tuple-element.86), channel_id=1, source_target_pairs={{0,192},{64,0},{128,64},{192,128},{1,193},{65,1},{129,65},{193,129... | collective-permute-start | bytes 1572872 | tf_op jit(solution)/shard_map/ppermute | solution.py:43
  140.1 22.5 %collective-permute-start.16 = (bf16[256,1024]{1,0:T(8,128)(2,1)S(1)}, bf16[256,1024]{1,0:T(8,128)(2,1)S(1)}, u32[]{:S(2)}, u32[]{:S(2)}) collective-permute-start(bf16[256,1024]{1,0:T(8,128)(2,1)S(1)} %collective-permute-done.14.refs_0_), channel_id=1, source_target_pairs={{0,192},{64,0},{128,64},{192,128},{1,193},{65,1},{129,65},{193,129... | collective-permute-start | bytes 1572872 | tf_op jit(solution)/shard_map/ppermute | solution.py:43
  141.7 20.9 %collective-permute-start.17 = (bf16[256,1024]{1,0:T(8,128)(2,1)S(1)}, bf16[256,1024]{1,0:T(8,128)(2,1)S(1)}, u32[]{:S(2)}, u32[]{:S(2)}) collective-permute-start(bf16[256,1024]{1,0:T(8,128)(2,1)S(1)} %collective-permute-done.15.refs_1_), channel_id=1, source_target_pairs={{0,64},{64,128},{128,192},{192,0},{1,65},{65,129},{129,193},{193,1... | collective-permute-start | bytes 1572872 | tf_op jit(solution)/shard_map/ppermute | solution.py:43
  149.5 28.8 %collective-permute-start.22 = (bf16[256,1024]{1,0:T(8,128)(2,1)S(1)}, bf16[256,1024]{1,0:T(8,128)(2,1)S(1)}, u32[]{:S(2)}, u32[]{:S(2)}) collective-permute-start(bf16[256,1024]{1,0:T(8,128)(2,1)S(1)} %get-tuple-element.65), channel_id=1, source_target_pairs={{0,64},{64,128},{128,192},{192,0},{1,65},{65,129},{129,193},{193,1... | collective-permute-start | bytes 1572872 | tf_op jit(solution)/shard_map/ppermute | solution.py:43
  151.6 26.7 %collective-permute-start.23 = (bf16[256,1024]{1,0:T(8,128)(2,1)S(1)}, bf16[256,1024]{1,0:T(8,128)(2,1)S(1)}, u32[]{:S(2)}, u32[]{:S(2)}) collective-permute-start(bf16[256,1024]{1,0:T(8,128)(2,1)S(1)} %get-tuple-element.66), channel_id=1, source_target_pairs={{0,192},{64,0},{128,64},{192,128},{1,193},{65,1},{129,65},{193,129... | collective-permute-start | bytes 1572872 | tf_op jit(solution)/shard_map/ppermute | solution.py:43
  168.8 14.4 %collective-permute-start.20 = (bf16[256,1024]{1,0:T(8,128)(2,1)S(1)}, bf16[256,1024]{1,0:T(8,128)(2,1)S(1)}, u32[]{:S(2)}, u32[]{:S(2)}) collective-permute-start(bf16[256,1024]{1,0:T(8,128)(2,1)S(1)} %get-tuple-element.69), channel_id=1, source_target_pairs={{0,192},{64,0},{128,64},{192,128},{1,193},{65,1},{129,65},{193,129... | collective-permute-start | bytes 1572872 | tf_op jit(solution)/shard_map/ppermute | solution.py:43
  170.4 12.8 %collective-permute-start.21 = (bf16[256,1024]{1,0:T(8,128)(2,1)S(1)}, bf16[256,1024]{1,0:T(8,128)(2,1)S(1)}, u32[]{:S(2)}, u32[]{:S(2)}) collective-permute-start(bf16[256,1024]{1,0:T(8,128)(2,1)S(1)} %get-tuple-element.70), channel_id=1, source_target_pairs={{0,64},{64,128},{128,192},{192,0},{1,65},{65,129},{129,193},{193,1... | collective-permute-start | bytes 1572872 | tf_op jit(solution)/shard_map/ppermute | solution.py:43
  183.4 12.3 %collective-permute-start.25 = (bf16[256,1024]{1,0:T(8,128)(2,1)S(1)}, bf16[256,1024]{1,0:T(8,128)(2,1)S(1)}, u32[]{:S(2)}, u32[]{:S(2)}) collective-permute-start(bf16[256,1024]{1,0:T(8,128)(2,1)S(1)} %add_convert_fusion), channel_id=1, source_target_pairs={{0,64},{64,128},{128,192},{192,0},{1,65},{65,129},{129,193},{193,1... | collective-permute-start | bytes 1572872 | tf_op jit(solution)/shard_map/ppermute | solution.py:43
  186.6 21.4 %copy-start.8 = (f32[8,8]{1,0:T(8,128)S(1)}, f32[8,8]{1,0:T(8,128)}, u32[]{:S(2)}) copy-start(f32[8,8]{1,0:T(8,128)} %param.29) | copy-start | bytes 772
  186.6 12.8 %collective-permute-start.24 = (bf16[256,1024]{1,0:T(8,128)(2,1)S(1)}, bf16[256,1024]{1,0:T(8,128)(2,1)S(1)}, u32[]{:S(2)}, u32[]{:S(2)}) collective-permute-start(bf16[256,1024]{1,0:T(8,128)(2,1)S(1)} %add_convert_fusion.1), channel_id=1, source_target_pairs={{0,192},{64,0},{128,64},{192,128},{1,193},{65,1},{129,65},{193,129... | collective-permute-start | bytes 1572872 | tf_op jit(solution)/shard_map/ppermute | solution.py:43
  200.6 36.2 %copy-start.3 = (bf16[8,4096]{1,0:T(8,128)(2,1)S(1)}, bf16[8,4096]{1,0:T(8,128)(2,1)}, u32[]{:S(2)}) copy-start(bf16[8,4096]{1,0:T(8,128)(2,1)} %get-tuple-element.40.attended_ref) | copy-start | bytes 196612
  200.6 36.2 %all-to-all-start.3 = ((bf16[64,8,1024]{2,1,0:T(8,128)(2,1)}), bf16[64,8,1024]{2,1,0:T(8,128)(2,1)S(1)}, u32[]{:S(2)}, u32[]{:S(2)}) async-start(bf16[64,8,1024]{2,1,0:T(8,128)(2,1)} %bitcast.27), calls=%async_computation.3 | async-start | bytes 2097152 | tf_op jit(solution)/shard_map/all_to_all | solution.py:454

commit v3 on v2

--- a/solution.py
+++ b/solution.py
@@ -463,10 +463,10 @@
     right_a, left_b, own = tie((right_a, left_b, own))
     far_a, far_b = shift_pool(right_a, -1), shift_pool(left_b, 1)
     to_right_a, to_left_b = expert([right_a, left_b], *weights, share=64)
-    from_left_a, from_right_b = shift_pool(to_right_a, 1), shift_pool(to_left_b, -1)
     far_a, far_b, left_a, right_b, to_right_a, to_left_b = tie(
         (far_a, far_b, left_a, right_b, to_right_a, to_left_b)
     )
+    from_left_a, from_right_b = shift_pool(to_right_a, 1), shift_pool(to_left_b, -1)
     to_far_a, to_far_b = expert([far_a, far_b], *weights)
     over_a, over_b = shift_pool(to_far_a, -1), shift_pool(to_far_b, 1)
     left_a, right_b, to_far_a, to_far_b = tie((left_a, right_b, to_far_a, to_far_b))

time: 239 us -> 241 us (level)
  waiting for transfers between devices: 82.8 us -> 86.7 us
    ppermute x18, waiting for transfers between devices: 34.2 us -> 38.6 us  [shift_pool(): lax.ppermute(value, 'pool', [(i, (i + step) % N_POOL) for i in range(N_PO...]
  transfers between devices with their start and end apart: 28 -> 28, of which waited for: 13 -> 17; matrix products, arithmetic and copies ran while one was open for 5% -> 5% of each run, Pallas kernels for 14% -> 14%
where the time goes in v3:
time: 241 us; the launch traced here: 240 us
  waiting for transfers between devices  86.7 us (36%)
  blocking collectives  51.7 us (21%)
  starting transfers between devices  47.2 us (20%)
  Pallas kernels  38.9 us (16%)
  local copies, waits for them, and re-layouts  7.92 us (3%)
  other arithmetic  6.23 us (3%)
    ppermute x18, waiting for transfers between devices, shift_pool(): lax.ppermute(value, 'pool', [(i, (i + step) % N_POOL) for i in range(N_PO...  38.6 us
    all_to_all x1, blocking collectives, exchange(): lax.all_to_all(parted, 'ep', split_axis=0, concat_axis=0, tiled=True)  34.5 us
    all_to_all x1, waiting for transfers between devices, exchange(): lax.all_to_all(parted, 'ep', split_axis=0, concat_axis=0, tiled=True)  27.2 us
    pallas_call x4, Pallas kernels, expert(): pl.pallas_call(functools.partial(expert_kernel, layout), grid=(2 * STEPS,...  24.6 us
    ppermute x18, starting transfers between devices, shift_pool(): lax.ppermute(value, 'pool', [(i, (i + step) % N_POOL) for i in range(N_PO...  24.4 us
    all_to_all x1, blocking collectives, project(): lax.all_to_all(context.reshape(N_Z, ROWS, DEEP), 'ep', split_axis=0, conc...  17.3 us
    all_to_all x1, waiting for transfers between devices, project(): lax.all_to_all(product.reshape(N_EP, ROWS, CHUNK), 'ep', split_axis=0, co...  14.3 us
    ppermute x8, starting transfers between devices, shift_ep(): return lax.ppermute(value, 'ep', pairs)  9.27 us
  transfers between devices with their start and end apart: 28, of which 17 were waited for; matrix products, arithmetic and copies ran while one was open for 5% of the time, Pallas kernels for 14%

profile of v3, /device:TPU:24, one launch (start us, length us, event | category | flops | bytes accessed | tf_op | source)
XLA Modules:
  0.0 239.6 jit_solution(3449811771147448607)
XLA Ops:
  0.7 1.3 dynamic-slice_bitcast_fusion
  2.0 0.7 add_select_fusion
  2.7 0.7 broadcast_compare_fusion.1
  3.6 0.5 slice_bitcast_fusion.2
  4.1 2.0 collective-permute-start
  6.0 0.9 collective-permute-start.1
  6.9 0.8 select_reduce_fusion.2
  7.7 0.7 pad_add_fusion
  8.4 0.6 reshape.156.facts_ref
  9.0 1.6 copy.46
  10.6 0.5 collective-permute-done.1.refs_2_
  11.1 0.6 collective-permute-done.2.refs_3_
  11.6 0.5 copy-done.12
  12.2 2.8 %shard_map.176 = (bf16[4,2,16,512]{3,2,1,0:T(8,128)(2,1)}, bf16[4,2,16,512]{3,2,1,0:T(8,128)(2,1)}, bf16[4,2,16,512]{3,2,1,0:T(8,128)(2,1)}, bf16[4,2,16,512]{3,2,1,0:T(8,128)(2,1)}) custom-call(s32[8]{0:T(128)} %get-tuple-element.44.refs_0_, s32[8]{0:T(128)} %copy-done.10, s32[8]{0:T(128)} %copy-done.11, s32[8]{0:T(128)} %copy-done.12, ...), custom_call_target="tpu_custom_call" | custom-call | bytes 1048576 | tf_op jit(solution)/shard_map/pallas_call | solution.py:105
  15.0 1.7 collective-permute-start.3
  16.7 2.1 collective-permute-start.5
  18.8 1.2 collective-permute-start.6
  20.3 2.4 collective-permute-done.3.b1
  22.7 1.1 collective-permute-start.7
  23.8 2.4 %collective-permute-start.8 = (bf16[256,512]{1,0:T(8,128)(2,1)S(1)}, bf16[256,512]{1,0:T(8,128)(2,1)S(1)}, u32[]{:S(2)}, u32[]{:S(2)}) collective-permute-start(bf16[256,512]{1,0:T(8,128)(2,1)S(1)} %get-tuple-element.93), channel_id=1, source_target_pairs={{0,4},{1,5},{2,6},{3,7},{4,0},{5,1},{6,2},{7,3},{8,12},{9,13},{10,... | collective-permute-start | bytes 786440 | tf_op jit(solution)/shard_map/ppermute | solution.py:51
  26.3 1.8 collective-permute-start.9
  28.1 0.6 copy-done.5
  28.8 5.4 %shard_map.177 = bf16[64,1024]{1,0:T(8,128)(2,1)} custom-call(s32[56]{0:T(128)} %reshape.156.facts_ref, bf16[8,64,128]{2,1,0:T(8,128)(2,1)} %bitcast.66, bf16[8,512]{1,0:T(8,128)(2,1)} %key_ref.1, bf16[8,512]{1,0:T(8,128)(2,1)} %value_ref.1, bf16[8,2,64,512]{3,2,1,0:T(8,128)(2,1)} %resident_ref.1, bf16[4,2,16,512]{3,2,1,0:T(8,128)(2,1)} %get-tuple-element.53.b0, ...), custom_call_target="tpu_custom_call" | custom-call | flops 268435456 | bytes 3145728 | tf_op jit(solution)/shard_map/pallas_call | solution.py:177
  34.2 17.3 %all_to_all.20 = bf16[8,8,1024]{2,1,0:T(8,128)(2,1)S(1)} all-to-all(bf16[8,8,1024]{2,1,0:T(8,128)(2,1)} %bitcast.67), channel_id=1, replica_groups={{0,8,16,24,32,40,48,56},{1,9,17,25,33,41,49,57},{2,10,18,26,34,42,50,58..., dimensions={0} | all-to-all | bytes 262144 | tf_op jit(solution)/shard_map/all_to_all | solution.py:240
  51.5 1.0 collective-permute-start.10
  52.5 1.0 collective-permute-start.11
  53.5 1.8 collective-permute-start.12
  55.3 3.9 %collective-permute-done.10.refs_1_ = bf16[64,1024]{1,0:T(8,128)(2,1)S(1)} collective-permute-done((bf16[64,1024]{1,0:T(8,128)(2,1)S(1)}, bf16[64,1024]{1,0:T(8,128)(2,1)S(1)}, u32[]{:S(2)}, u32[]{:S(2)}) %collective-permute-start.10) | collective-permute-done | bytes 131104 | tf_op jit(solution)/shard_map/ppermute | solution.py:51
  59.2 0.9 collective-permute-done.12.refs_3_
  60.3 1.8 collective-permute-done.13.other_ref
  62.1 2.1 shard_map.179
  64.1 5.7 %all-to-all-start.1 = ((bf16[64,8,512]{2,1,0:T(8,128)(2,1)}), bf16[64,8,512]{2,1,0:T(8,128)(2,1)}, u32[]{:S(2)}, u32[]{:S(2)}) async-start(bf16[64,8,512]{2,1,0:T(8,128)(2,1)} %bitcast.16), calls=%async_computation.1 | async-start | bytes 1048576 | tf_op jit(solution)/shard_map/all_to_all | solution.py:264
  70.4 1.2 select_convert_fusion
  71.6 1.4 convert_element_type.37.pick_ref
  73.0 14.3 %all-to-all-done.1 = bf16[64,8,512]{2,1,0:T(8,128)(2,1)} async-done(((bf16[64,8,512]{2,1,0:T(8,128)(2,1)}), bf16[64,8,512]{2,1,0:T(8,128)(2,1)}, u32[]{:S(2)}, u32[]{:S(2)}) %all-to-all-start.1) | async-done | bytes 524320 | tf_op jit(solution)/shard_map/all_to_all | solution.py:264
  87.3 1.8 shard_map.180
  89.1 34.5 %all_to_all.21 = bf16[64,8,1024]{2,1,0:T(8,128)(2,1)S(1)} all-to-all(bf16[64,8,1024]{2,1,0:T(8,128)(2,1)S(1)} %bitcast.50), channel_id=1, replica_groups=mesh['pool'=4,'ep'=64] {'ep'}, dimensions={0} | all-to-all | bytes 2097152 | tf_op jit(solution)/shard_map/all_to_all | solution.py:454
  123.7 3.2 %collective-permute-start.15 = (bf16[256,1024]{1,0:T(8,128)(2,1)S(1)}, bf16[256,1024]{1,0:T(8,128)(2,1)S(1)}, u32[]{:S(2)}, u32[]{:S(2)}) collective-permute-start(bf16[256,1024]{1,0:T(8,128)(2,1)S(1)} %get-tuple-element.90), channel_id=1, source_target_pairs={{0,64},{64,128},{128,192},{192,0},{1,65},{65,129},{129,193},{193,1... | collective-permute-start | bytes 1572872 | tf_op jit(solution)/shard_map/ppermute | solution.py:43
  126.9 1.3 collective-permute-start.18
  128.2 0.7 collective-permute-start.19
  128.9 6.2 %shard_map.181 = bf16[512,1024]{1,0:T(8,128)(2,1)S(1)} custom-call(bf16[256,256]{1,0:T(8,128)(2,1)S(1)} %copy-done.1, bf16[512,1024]{1,0:T(8,128)(2,1)S(1)} %bitcast.48, bf16[4096,384]{1,0:T(8,128)(2,1)S(1)} %bitcast.44, bf16[4096,384]{1,0:T(8,128)(2,1)} %bitcast.55, bf16[384,4096]{1,0:T(8,128)(2,1)} %bitcast.59), custom_call_target="tpu_custom_call" | custom-call | flops 1207959552 | bytes 11534336 | tf_op jit(solution)/shard_map/pallas_call | solution.py:346
  135.1 4.6 %collective-permute-done.14.refs_0_ = bf16[256,1024]{1,0:T(8,128)(2,1)S(1)} collective-permute-done((bf16[256,1024]{1,0:T(8,128)(2,1)S(1)}, bf16[256,1024]{1,0:T(8,128)(2,1)S(1)}, u32[]{:S(2)}, u32[]{:S(2)}) %collective-permute-start.14) | collective-permute-done | bytes 524320 | tf_op jit(solution)/shard_map/ppermute | solution.py:43
  139.8 0.6 collective-permute-done.15.refs_1_
  140.3 2.0 collective-permute-start.16
  142.4 1.2 collective-permute-start.17
  143.6 6.2 %shard_map.182 = (bf16[256,1024]{1,0:T(8,128)(2,1)S(1)}, bf16[256,1024]{1,0:T(8,128)(2,1)S(1)}) custom-call(bf16[256,256]{1,0:T(8,128)(2,1)S(1)} %copy-done.1, bf16[256,1024]{1,0:T(8,128)(2,1)S(1)} %collective-permute-done.14.refs_0_, bf16[256,1024]{1,0:T(8,128)(2,1)S(1)} %collective-permute-done.15.refs_1_, bf16[4096,384]{1,0:T(8,128)(2,1)S(1)} %bitcast.45, ...), custom_call_target="tpu_custom_call" | custom-call | flops 18874368 | bytes 180224 | tf_op jit(solution)/shard_map/pallas_call | solution.py:346
  149.7 1.8 collective-permute-done.18.refs_0_
  151.6 8.8 %collective-permute-done.16.refs_0_ = bf16[256,1024]{1,0:T(8,128)(2,1)S(1)} collective-permute-done((bf16[256,1024]{1,0:T(8,128)(2,1)S(1)}, bf16[256,1024]{1,0:T(8,128)(2,1)S(1)}, u32[]{:S(2)}, u32[]{:S(2)}) %collective-permute-start.16) | collective-permute-done | bytes 524320 | tf_op jit(solution)/shard_map/ppermute | solution.py:43
  160.3 0.6 collective-permute-done.17.refs_1_
  160.9 2.4 collective-permute-start.22
  163.3 6.2 %shard_map.183 = (bf16[256,1024]{1,0:T(8,128)(2,1)S(1)}, bf16[256,1024]{1,0:T(8,128)(2,1)S(1)}) custom-call(bf16[256,256]{1,0:T(8,128)(2,1)S(1)} %copy-done.1, bf16[256,1024]{1,0:T(8,128)(2,1)S(1)} %collective-permute-done.16.refs_0_, bf16[256,1024]{1,0:T(8,128)(2,1)S(1)} %collective-permute-done.17.refs_1_, bf16[4096,384]{1,0:T(8,128)(2,1)S(1)} %bitcast.46, ...), custom_call_target="tpu_custom_call" | custom-call | flops 1207959552 | bytes 11534336 | tf_op jit(solution)/shard_map/pallas_call | solution.py:346
  169.5 1.5 collective-permute-start.20
  170.9 1.9 collective-permute-start.21
  172.9 6.2 %shard_map.184 = (bf16[256,1024]{1,0:T(8,128)(2,1)S(1)}, bf16[256,1024]{1,0:T(8,128)(2,1)S(1)}) custom-call(bf16[256,256]{1,0:T(8,128)(2,1)S(1)} %copy-done.1, bf16[256,1024]{1,0:T(8,128)(2,1)S(1)} %collective-permute-done.18.refs_0_, bf16[256,1024]{1,0:T(8,128)(2,1)S(1)} %collective-permute-done.19.refs_1_, bf16[4096,384]{1,0:T(8,128)(2,1)S(1)} %bitcast.47, ...), custom_call_target="tpu_custom_call" | custom-call | flops 1207959552 | bytes 11534336 | tf_op jit(solution)/shard_map/pallas_call | solution.py:346
  179.8 7.5 %collective-permute-done.20 = bf16[256,1024]{1,0:T(8,128)(2,1)S(1)} collective-permute-done((bf16[256,1024]{1,0:T(8,128)(2,1)S(1)}, bf16[256,1024]{1,0:T(8,128)(2,1)S(1)}, u32[]{:S(2)}, u32[]{:S(2)}) %collective-permute-start.20) | collective-permute-done | bytes 524320 | tf_op jit(solution)/shard_map/ppermute | solution.py:43
  188.0 1.8 collective-permute-start.24
  189.8 8.3 %collective-permute-done.25.more_b_ref = bf16[256,1024]{1,0:T(8,128)(2,1)S(1)} collective-permute-done((bf16[256,1024]{1,0:T(8,128)(2,1)S(1)}, bf16[256,1024]{1,0:T(8,128)(2,1)S(1)}, u32[]{:S(2)}, u32[]{:S(2)}) %collective-permute-start.25) | collective-permute-done | bytes 524320 | tf_op jit(solution)/shard_map/ppermute | solution.py:43
  198.1 2.7 %collective-permute-done.24.more_a_ref = bf16[256,1024]{1,0:T(8,128)(2,1)S(1)} collective-permute-done((bf16[256,1024]{1,0:T(8,128)(2,1)S(1)}, bf16[256,1024]{1,0:T(8,128)(2,1)S(1)}, u32[]{:S(2)}, u32[]{:S(2)}) %collective-permute-start.24) | collective-permute-done | bytes 524320 | tf_op jit(solution)/shard_map/ppermute | solution.py:43
  200.8 1.1 shard_map.185
  201.9 7.8 %all-to-all-start.3 = ((bf16[64,8,1024]{2,1,0:T(8,128)(2,1)}), bf16[64,8,1024]{2,1,0:T(8,128)(2,1)S(1)}, u32[]{:S(2)}, u32[]{:S(2)}) async-start(bf16[64,8,1024]{2,1,0:T(8,128)(2,1)} %bitcast.27), calls=%async_computation.3 | async-start | bytes 2097152 | tf_op jit(solution)/shard_map/all_to_all | solution.py:454
  210.4 0.4 and_select_fusion
  210.9 0.5 select_n.156
  211.5 27.2 %all-to-all-done.3 = bf16[64,8,1024]{2,1,0:T(8,128)(2,1)S(1)} async-done(((bf16[64,8,1024]{2,1,0:T(8,128)(2,1)}), bf16[64,8,1024]{2,1,0:T(8,128)(2,1)S(1)}, u32[]{:S(2)}, u32[]{:S(2)}) %all-to-all-start.3) | async-done | bytes 1048608 | tf_op jit(solution)/shard_map/all_to_all | solution.py:454
  238.7 0.9 shard_map.186
  (74 shorter events, 3.9 us)
Async XLA Ops:
  1.9 18.2 %collective-permute-start.4 = (bf16[128,2048]{1,0:T(8,128)(2,1)S(1)}, bf16[128,2048]{1,0:T(8,128)(2,1)S(1)}, u32[]{:S(2)}, u32[]{:S(2)}) collective-permute-start(bf16[128,2048]{1,0:T(8,128)(2,1)S(1)} %get-tuple-element.97), channel_id=1, source_target_pairs={{0,1},{1,0},{2,3},{3,2},{4,5},{5,4},{6,7},{7,6},{8,9},{9,8},{10,11... | collective-permute-start | bytes 1572872 | tf_op jit(solution)/shard_map/ppermute | solution.py:51
  4.1 6.5 %collective-permute-start = (s32[8]{0:T(128)S(1)}, s32[8]{0:T(128)S(1)}, u32[]{:S(2)}, u32[]{:S(2)}) collective-permute-start(s32[8]{0:T(128)S(1)} %get-tuple-element.103), channel_id=1, source_target_pairs={{0,64},{64,128},{128,192},{192,0},{1,65},{65,129},{129,193},{193,1... | collective-permute-start | bytes 104 | tf_op jit(solution)/shard_map/ppermute | solution.py:43
  6.0 5.0 %collective-permute-start.1 = (s32[8]{0:T(128)S(1)}, s32[8]{0:T(128)S(1)}, u32[]{:S(2)}, u32[]{:S(2)}) collective-permute-start(s32[8]{0:T(128)S(1)} %get-tuple-element.102), channel_id=1, source_target_pairs={{0,128},{64,192},{128,0},{192,64},{1,129},{65,193},{129,1},{193,65... | collective-permute-start | bytes 104 | tf_op jit(solution)/shard_map/ppermute | solution.py:43
  6.9 4.8 %collective-permute-start.2 = (s32[8]{0:T(128)S(1)}, s32[8]{0:T(128)S(1)}, u32[]{:S(2)}, u32[]{:S(2)}) collective-permute-start(s32[8]{0:T(128)S(1)} %get-tuple-element.101), channel_id=1, source_target_pairs={{0,192},{64,0},{128,64},{192,128},{1,193},{65,1},{129,65},{193,129... | collective-permute-start | bytes 104 | tf_op jit(solution)/shard_map/ppermute | solution.py:43
  10.6 1.1 copy-start.10
  11.1 0.6 copy-start.11
  11.6 0.5 copy-start.12
  15.0 7.6 %collective-permute-start.3 = (bf16[4,2,16,512]{3,2,1,0:T(8,128)(2,1)}, bf16[4,2,16,512]{3,2,1,0:T(8,128)(2,1)S(1)}, u32[]{:S(2)}, u32[]{:S(2)}) collective-permute-start(bf16[4,2,16,512]{3,2,1,0:T(8,128)(2,1)} %get-tuple-element.48), channel_id=1, source_target_pairs={{0,192},{64,0},{128,64},{192,128},{1,193},{65,1},{129,65},{193,129... | collective-permute-start | bytes 393224 | tf_op jit(solution)/shard_map/ppermute | solution.py:43
  16.7 11.3 %collective-permute-start.5 = (bf16[4,2,16,512]{3,2,1,0:T(8,128)(2,1)}, bf16[4,2,16,512]{3,2,1,0:T(8,128)(2,1)S(1)}, u32[]{:S(2)}, u32[]{:S(2)}) collective-permute-start(bf16[4,2,16,512]{3,2,1,0:T(8,128)(2,1)} %get-tuple-element.55), channel_id=1, source_target_pairs={{0,128},{64,192},{128,0},{192,64},{1,129},{65,193},{129,1},{193,65... | collective-permute-start | bytes 393224 | tf_op jit(solution)/shard_map/ppermute | solution.py:43
  18.8 9.2 %collective-permute-start.6 = (bf16[4,2,16,512]{3,2,1,0:T(8,128)(2,1)}, bf16[4,2,16,512]{3,2,1,0:T(8,128)(2,1)S(1)}, u32[]{:S(2)}, u32[]{:S(2)}) collective-permute-start(bf16[4,2,16,512]{3,2,1,0:T(8,128)(2,1)} %get-tuple-element.56), channel_id=1, source_target_pairs={{0,64},{64,128},{128,192},{192,0},{1,65},{65,129},{129,193},{193,1... | collective-permute-start | bytes 393224 | tf_op jit(solution)/shard_map/ppermute | solution.py:43
  22.6 5.5 %copy-start.4 = (bf16[4,2,16,512]{3,2,1,0:T(8,128)(2,1)}, bf16[4,2,16,512]{3,2,1,0:T(8,128)(2,1)S(1)}, u32[]{:S(2)}) copy-start(bf16[4,2,16,512]{3,2,1,0:T(8,128)(2,1)S(1)} %collective-permute-done.3.b1) | copy-start | bytes 393220
  22.7 28.8 %collective-permute-start.7 = (bf16[256,512]{1,0:T(8,128)(2,1)S(1)}, bf16[256,512]{1,0:T(8,128)(2,1)S(1)}, u32[]{:S(2)}, u32[]{:S(2)}) collective-permute-start(bf16[256,512]{1,0:T(8,128)(2,1)S(1)} %get-tuple-element.94), channel_id=1, source_target_pairs={{0,2},{1,3},{2,4},{3,5},{4,6},{5,7},{6,0},{7,1},{8,10},{9,11},{10,... | collective-permute-start | bytes 786440 | tf_op jit(solution)/shard_map/ppermute | solution.py:51
  23.8 27.7 %collective-permute-start.8 = (bf16[256,512]{1,0:T(8,128)(2,1)S(1)}, bf16[256,512]{1,0:T(8,128)(2,1)S(1)}, u32[]{:S(2)}, u32[]{:S(2)}) collective-permute-start(bf16[256,512]{1,0:T(8,128)(2,1)S(1)} %get-tuple-element.93), channel_id=1, source_target_pairs={{0,4},{1,5},{2,6},{3,7},{4,0},{5,1},{6,2},{7,3},{8,12},{9,13},{10,... | collective-permute-start | bytes 786440 | tf_op jit(solution)/shard_map/ppermute | solution.py:51
  26.3 25.2 %collective-permute-start.9 = (bf16[256,512]{1,0:T(8,128)(2,1)S(1)}, bf16[256,512]{1,0:T(8,128)(2,1)S(1)}, u32[]{:S(2)}, u32[]{:S(2)}) collective-permute-start(bf16[256,512]{1,0:T(8,128)(2,1)S(1)} %get-tuple-element.92), channel_id=1, source_target_pairs={{0,6},{1,7},{2,0},{3,1},{4,2},{5,3},{6,4},{7,5},{8,14},{9,15},{10,... | collective-permute-start | bytes 786440 | tf_op jit(solution)/shard_map/ppermute | solution.py:51
  28.1 0.7 copy-start.5
  28.1 0.7 copy-start.6
  28.8 41.1 %copy-start.7 = (s32[8,8]{1,0:T(8,128)S(1)}, s32[8,8]{1,0:T(8,128)}, u32[]{:S(2)}) copy-start(s32[8,8]{1,0:T(8,128)} %param.28) | copy-start | bytes 772
  34.2 38.7 %copy-start.9 = (bf16[4096]{0:T(1024)(128)(2,1)S(1)}, bf16[4096]{0:T(1024)(128)(2,1)}, u32[]{:S(2)}) copy-start(bf16[4096]{0:T(1024)(128)(2,1)} %param.27) | copy-start | bytes 24580
  34.2 53.1 %copy-start.2 = (bf16[8,4096]{1,0:T(8,128)(2,1)S(1)}, bf16[8,4096]{1,0:T(8,128)(2,1)}, u32[]{:S(2)}) copy-start(bf16[8,4096]{1,0:T(8,128)(2,1)} %residual_ref.1) | copy-start | bytes 196612
  51.5 7.7 %collective-permute-start.10 = (bf16[64,1024]{1,0:T(8,128)(2,1)S(1)}, bf16[64,1024]{1,0:T(8,128)(2,1)S(1)}, u32[]{:S(2)}, u32[]{:S(2)}) collective-permute-start(bf16[64,1024]{1,0:T(8,128)(2,1)S(1)} %bitcast.51), channel_id=1, source_target_pairs={{0,2},{1,3},{2,4},{3,5},{4,6},{5,7},{6,0},{7,1},{8,10},{9,11},{10,... | collective-permute-start | bytes 393224 | tf_op jit(solution)/shard_map/ppermute | solution.py:51
  52.5 6.7 %collective-permute-start.11 = (bf16[64,1024]{1,0:T(8,128)(2,1)S(1)}, bf16[64,1024]{1,0:T(8,128)(2,1)S(1)}, u32[]{:S(2)}, u32[]{:S(2)}) collective-permute-start(bf16[64,1024]{1,0:T(8,128)(2,1)S(1)} %bitcast.52), channel_id=1, source_target_pairs={{0,4},{1,5},{2,6},{3,7},{4,0},{5,1},{6,2},{7,3},{8,12},{9,13},{10,... | collective-permute-start | bytes 393224 | tf_op jit(solution)/shard_map/ppermute | solution.py:51
  53.5 6.6 %collective-permute-start.12 = (bf16[64,1024]{1,0:T(8,128)(2,1)S(1)}, bf16[64,1024]{1,0:T(8,128)(2,1)S(1)}, u32[]{:S(2)}, u32[]{:S(2)}) collective-permute-start(bf16[64,1024]{1,0:T(8,128)(2,1)S(1)} %bitcast.53), channel_id=1, source_target_pairs={{0,6},{1,7},{2,0},{3,1},{4,2},{5,3},{6,4},{7,5},{8,14},{9,15},{10,... | collective-permute-start | bytes 393224 | tf_op jit(solution)/shard_map/ppermute | solution.py:51
  60.1 2.0 collective-permute-start.13
  64.1 23.2 %all-to-all-start.1 = ((bf16[64,8,512]{2,1,0:T(8,128)(2,1)}), bf16[64,8,512]{2,1,0:T(8,128)(2,1)}, u32[]{:S(2)}, u32[]{:S(2)}) async-start(bf16[64,8,512]{2,1,0:T(8,128)(2,1)} %bitcast.16), calls=%async_computation.1 | async-start | bytes 1048576 | tf_op jit(solution)/shard_map/all_to_all | solution.py:264
  70.1 58.8 %copy-start = (bf16[1,4096,384]{2,1,0:T(8,128)(2,1)S(1)}, bf16[1,4096,384]{2,1,0:T(8,128)(2,1)}, u32[]{:S(2)}) copy-start(bf16[1,4096,384]{2,1,0:T(8,128)(2,1)} %param.30) | copy-start | bytes 9437188
  70.1 58.9 %copy-start.1 = (bf16[256,256]{1,0:T(8,128)(2,1)S(1)}, bf16[256,256]{1,0:T(8,128)(2,1)}, u32[]{:S(2)}) copy-start(bf16[256,256]{1,0:T(8,128)(2,1)} %constant.113.clone.order_ref) | copy-start | bytes 393220
  123.6 16.2 %collective-permute-start.14 = (bf16[256,1024]{1,0:T(8,128)(2,1)S(1)}, bf16[256,1024]{1,0:T(8,128)(2,1)S(1)}, u32[]{:S(2)}, u32[]{:S(2)}) collective-permute-start(bf16[256,1024]{1,0:T(8,128)(2,1)S(1)} %get-tuple-element.91), channel_id=1, source_target_pairs={{0,192},{64,0},{128,64},{192,128},{1,193},{65,1},{129,65},{193,129... | collective-permute-start | bytes 1572872 | tf_op jit(solution)/shard_map/ppermute | solution.py:43
  123.7 16.6 %collective-permute-start.15 = (bf16[256,1024]{1,0:T(8,128)(2,1)S(1)}, bf16[256,1024]{1,0:T(8,128)(2,1)S(1)}, u32[]{:S(2)}, u32[]{:S(2)}) collective-permute-start(bf16[256,1024]{1,0:T(8,128)(2,1)S(1)} %get-tuple-element.90), channel_id=1, source_target_pairs={{0,64},{64,128},{128,192},{192,0},{1,65},{65,129},{129,193},{193,1... | collective-permute-start | bytes 1572872 | tf_op jit(solution)/shard_map/ppermute | solution.py:43
  126.9 24.7 %collective-permute-start.18 = (bf16[256,1024]{1,0:T(8,128)(2,1)S(1)}, bf16[256,1024]{1,0:T(8,128)(2,1)S(1)}, u32[]{:S(2)}, u32[]{:S(2)}) collective-permute-start(bf16[256,1024]{1,0:T(8,128)(2,1)S(1)} %get-tuple-element.91), channel_id=1, source_target_pairs={{0,64},{64,128},{128,192},{192,0},{1,65},{65,129},{129,193},{193,1... | collective-permute-start | bytes 1572872 | tf_op jit(solution)/shard_map/ppermute | solution.py:43
  128.2 23.4 %collective-permute-start.19 = (bf16[256,1024]{1,0:T(8,128)(2,1)S(1)}, bf16[256,1024]{1,0:T(8,128)(2,1)S(1)}, u32[]{:S(2)}, u32[]{:S(2)}) collective-permute-start(bf16[256,1024]{1,0:T(8,128)(2,1)S(1)} %get-tuple-element.90), channel_id=1, source_target_pairs={{0,192},{64,0},{128,64},{192,128},{1,193},{65,1},{129,65},{193,129... | collective-permute-start | bytes 1572872 | tf_op jit(solution)/shard_map/ppermute | solution.py:43
  140.3 20.0 %collective-permute-start.16 = (bf16[256,1024]{1,0:T(8,128)(2,1)S(1)}, bf16[256,1024]{1,0:T(8,128)(2,1)S(1)}, u32[]{:S(2)}, u32[]{:S(2)}) collective-permute-start(bf16[256,1024]{1,0:T(8,128)(2,1)S(1)} %collective-permute-done.14.refs_0_), channel_id=1, source_target_pairs={{0,192},{64,0},{128,64},{192,128},{1,193},{65,1},{129,65},{193,129... | collective-permute-start | bytes 1572872 | tf_op jit(solution)/shard_map/ppermute | solution.py:43
  142.4 18.6 %collective-permute-start.17 = (bf16[256,1024]{1,0:T(8,128)(2,1)S(1)}, bf16[256,1024]{1,0:T(8,128)(2,1)S(1)}, u32[]{:S(2)}, u32[]{:S(2)}) collective-permute-start(bf16[256,1024]{1,0:T(8,128)(2,1)S(1)} %collective-permute-done.15.refs_1_), channel_id=1, source_target_pairs={{0,64},{64,128},{128,192},{192,0},{1,65},{65,129},{129,193},{193,1... | collective-permute-start | bytes 1572872 | tf_op jit(solution)/shard_map/ppermute | solution.py:43
  160.9 18.1 %collective-permute-start.22 = (bf16[256,1024]{1,0:T(8,128)(2,1)S(1)}, bf16[256,1024]{1,0:T(8,128)(2,1)S(1)}, u32[]{:S(2)}, u32[]{:S(2)}) collective-permute-start(bf16[256,1024]{1,0:T(8,128)(2,1)S(1)} %get-tuple-element.74), channel_id=1, source_target_pairs={{0,64},{64,128},{128,192},{192,0},{1,65},{65,129},{129,193},{193,1... | collective-permute-start | bytes 1572872 | tf_op jit(solution)/shard_map/ppermute | solution.py:43
  163.3 16.1 %collective-permute-start.23 = (bf16[256,1024]{1,0:T(8,128)(2,1)S(1)}, bf16[256,1024]{1,0:T(8,128)(2,1)S(1)}, u32[]{:S(2)}, u32[]{:S(2)}) collective-permute-start(bf16[256,1024]{1,0:T(8,128)(2,1)S(1)} %get-tuple-element.75), channel_id=1, source_target_pairs={{0,192},{64,0},{128,64},{192,128},{1,193},{65,1},{129,65},{193,129... | collective-permute-start | bytes 1572872 | tf_op jit(solution)/shard_map/ppermute | solution.py:43
  169.5 17.8 %collective-permute-start.20 = (bf16[256,1024]{1,0:T(8,128)(2,1)S(1)}, bf16[256,1024]{1,0:T(8,128)(2,1)S(1)}, u32[]{:S(2)}, u32[]{:S(2)}) collective-permute-start(bf16[256,1024]{1,0:T(8,128)(2,1)S(1)} %get-tuple-element.71), channel_id=1, source_target_pairs={{0,192},{64,0},{128,64},{192,128},{1,193},{65,1},{129,65},{193,129... | collective-permute-start | bytes 1572872 | tf_op jit(solution)/shard_map/ppermute | solution.py:43
  170.9 16.3 %collective-permute-start.21 = (bf16[256,1024]{1,0:T(8,128)(2,1)S(1)}, bf16[256,1024]{1,0:T(8,128)(2,1)S(1)}, u32[]{:S(2)}, u32[]{:S(2)}) collective-permute-start(bf16[256,1024]{1,0:T(8,128)(2,1)S(1)} %get-tuple-element.72), channel_id=1, source_target_pairs={{0,64},{64,128},{128,192},{192,0},{1,65},{65,129},{129,193},{193,1... | collective-permute-start | bytes 1572872 | tf_op jit(solution)/shard_map/ppermute | solution.py:43
  187.4 10.7 %collective-permute-start.25 = (bf16[256,1024]{1,0:T(8,128)(2,1)S(1)}, bf16[256,1024]{1,0:T(8,128)(2,1)S(1)}, u32[]{:S(2)}, u32[]{:S(2)}) collective-permute-start(bf16[256,1024]{1,0:T(8,128)(2,1)S(1)} %add_convert_fusion), channel_id=1, source_target_pairs={{0,64},{64,128},{128,192},{192,0},{1,65},{65,129},{129,193},{193,1... | collective-permute-start | bytes 1572872 | tf_op jit(solution)/shard_map/ppermute | solution.py:43
  188.0 22.0 %copy-start.8 = (f32[8,8]{1,0:T(8,128)S(1)}, f32[8,8]{1,0:T(8,128)}, u32[]{:S(2)}) copy-start(f32[8,8]{1,0:T(8,128)} %param.29) | copy-start | bytes 772
  188.0 12.8 %collective-permute-start.24 = (bf16[256,1024]{1,0:T(8,128)(2,1)S(1)}, bf16[256,1024]{1,0:T(8,128)(2,1)S(1)}, u32[]{:S(2)}, u32[]{:S(2)}) collective-permute-start(bf16[256,1024]{1,0:T(8,128)(2,1)S(1)} %add_convert_fusion.1), channel_id=1, source_target_pairs={{0,192},{64,0},{128,64},{192,128},{1,193},{65,1},{129,65},{193,129... | collective-permute-start | bytes 1572872 | tf_op jit(solution)/shard_map/ppermute | solution.py:43
  201.9 36.7 %copy-start.3 = (bf16[8,4096]{1,0:T(8,128)(2,1)S(1)}, bf16[8,4096]{1,0:T(8,128)(2,1)}, u32[]{:S(2)}) copy-start(bf16[8,4096]{1,0:T(8,128)(2,1)} %get-tuple-element.42.attended_ref) | copy-start | bytes 196612
  201.9 36.7 %all-to-all-start.3 = ((bf16[64,8,1024]{2,1,0:T(8,128)(2,1)}), bf16[64,8,1024]{2,1,0:T(8,128)(2,1)S(1)}, u32[]{:S(2)}, u32[]{:S(2)}) async-start(bf16[64,8,1024]{2,1,0:T(8,128)(2,1)} %bitcast.27), calls=%async_computation.3 | async-start | bytes 2097152 | tf_op jit(solution)/shard_map/all_to_all | solution.py:454
